TPU v7x, 32 devices: a whole 2x2x4 slice. The times are simulated.
32 devices in a mesh: nodes: 8 (over z, y), mp: 4 (over x, core).
Axes of the slice: x: 2, y: 2, z: 4, core: 2. Of those that a mesh axis runs over, the one named last changes fastest.
Arguments:
- event_feats: bfloat16 [8192, 512], P('nodes'), may hold values from -6 to 6
- event_owner: int32 [8192, 1], P('nodes'), may hold values from 0 to 7; in each aligned block of 1024 rows (0 to 1023, 1024 to 2047, ...) at most 256 rows name the same one
- event_slot: int32 [8192], P('nodes'), may hold values from 0 to 255
- memory: bfloat16 [2048, 1024], P('nodes'), may hold values from -6 to 6
- w_msg_event: bfloat16 [512, 2048], P(None, 'mp'), may hold values from -0.25 to 0.25
- w_msg_state: bfloat16 [1024, 2048], P(None, 'mp'), may hold values from -0.1875 to 0.1875
- b_msg: float32 [2048], P('mp'), may hold values from -3 to 3
- w_msg_out: bfloat16 [2048, 1024], P('mp'), may hold values from -0.125 to 0.125
- b_out: float32 [1024], replicated, may hold values from -3 to 3
- w_input: bfloat16 [3, 1024, 1024], P(None, None, 'mp'), may hold values from -0.1875 to 0.1875
- w_hidden: bfloat16 [3, 1024, 1024], P(None, None, 'mp'), may hold values from -0.1875 to 0.1875
- b_input: float32 [3, 1024], P(None, 'mp'), may hold values from -3 to 3
- b_hidden: float32 [3, 1024], P(None, 'mp'), may hold values from -3 to 3
- state_slots: int32 [64, 32], P('nodes'), may hold values from 0 to 255
- neighbours: int32 [2048, 10], P('nodes'), may hold values from 0 to 255
- query_slots: int32 [2048], P('nodes'), may hold values from 0 to 255
- w_neigh: bfloat16 [1024, 1024], P('mp'), may hold values from -0.1875 to 0.1875
- w_self: bfloat16 [1024, 1024], P('mp'), may hold values from -0.1875 to 0.1875
- b_embed: float32 [1024], replicated, may hold values from -3 to 3
Outputs:
- new_memory: bfloat16 [2048, 1024], P('nodes', 'mp')
- embedding: bfloat16 [2048, 1024], P(('nodes', 'mp'))
Inputs may be any that keep to these rules, and one draw needn't show every extreme that they name: `event_owner`: among the 1024 events of one block of events, at most 256 name the same owner, and in every draw some owner is named exactly 256 times by some block.
All inputs are finite; a program needn't handle non-finite values.
Results may differ from a plain program's by a relative error of at most 0.014.
Values may be sent and summed in bfloat16 or wider, within the bound.
A program may use at most 64 MiB of HBM per device.

v0:
```python
import jax
import jax.numpy as jnp
from jax import lax
from jax.sharding import PartitionSpec as P


def per_device(
    event_feats,
    event_owner,
    event_slot,
    memory,
    w_msg_event,
    w_msg_state,
    b_msg,
    w_msg_out,
    b_out,
    w_input,
    w_hidden,
    b_input,
    b_hidden,
    state_slots,
    neighbours,
    query_slots,
    w_neigh,
    w_self,
    b_embed,
):
    owner_count = lax.axis_size("nodes")
    share_count = lax.axis_size("mp")
    mp_index = lax.axis_index("mp")
    event_rows = event_feats.shape[0]
    feat_width = event_feats.shape[1]
    mem_rows = memory.shape[0]
    mem_width = memory.shape[1]
    col_share = mem_width // share_count
    capacity = 2 * event_rows // owner_count
    owner = event_owner[:, 0]
    match = (owner[:, None] == lax.broadcasted_iota(jnp.int32, (1, owner_count), 1)).astype(
        jnp.int32
    )
    before = jnp.cumsum(match, axis=0) - match
    place = jnp.sum(before * match, axis=1)
    target = owner * capacity + place
    id_buffer = jnp.full((owner_count * capacity,), -1, jnp.int32).at[target].set(event_slot)
    id_buffer = id_buffer.reshape(owner_count, capacity)
    feat_buffer = (
        jnp.zeros((owner_count * capacity, feat_width), jnp.bfloat16).at[target].set(event_feats)
    )
    feat_buffer = feat_buffer.reshape(owner_count, capacity, feat_width)
    arrived = lax.all_to_all(feat_buffer, "nodes", split_axis=0, concat_axis=0, tiled=True)
    arrived_ids = lax.all_to_all(id_buffer, "nodes", split_axis=0, concat_axis=0, tiled=True)
    recv_rows = owner_count * capacity
    arrived = arrived.reshape(recv_rows, feat_width)
    arrived_ids = arrived_ids.reshape(recv_rows)
    valid = arrived_ids >= 0
    safe_ids = jnp.where(valid, arrived_ids, 0)
    segment_ids = jnp.where(valid, arrived_ids, mem_rows)
    state_proj = jnp.dot(memory, w_msg_state, preferred_element_type=jnp.float32)
    pre = (
        jnp.dot(arrived, w_msg_event, preferred_element_type=jnp.float32)
        + jnp.take(state_proj, safe_ids, axis=0)
        + b_msg
    )
    hidden_msg = jax.nn.relu(pre).astype(jnp.bfloat16)
    hidden_sum = jax.ops.segment_sum(
        hidden_msg.astype(jnp.float32), segment_ids, num_segments=mem_rows + 1
    )[:mem_rows]
    sum_head = hidden_sum.astype(jnp.bfloat16)
    sum_tail = (hidden_sum - sum_head.astype(jnp.float32)).astype(jnp.bfloat16)
    partial_total = jnp.dot(sum_head, w_msg_out, preferred_element_type=jnp.float32) + jnp.dot(
        sum_tail, w_msg_out, preferred_element_type=jnp.float32
    )
    counts = jax.ops.segment_sum(valid.astype(jnp.float32), segment_ids, num_segments=mem_rows + 1)[
        :mem_rows
    ]
    divisor = jnp.maximum(counts, 1.0)[:, None]
    msg_total = lax.psum(partial_total.astype(jnp.bfloat16), "mp").astype(jnp.float32)
    aggregate = (msg_total / divisor + b_out).astype(jnp.bfloat16)
    gates_in = (
        jnp.einsum("nd,gdc->gnc", aggregate, w_input, preferred_element_type=jnp.float32)
        + b_input[:, None, :]
    )
    gates_st = (
        jnp.einsum("nd,gdc->gnc", memory, w_hidden, preferred_element_type=jnp.float32)
        + b_hidden[:, None, :]
    )
    reset_gate = jax.nn.sigmoid(gates_in[0] + gates_st[0])
    update_gate = jax.nn.sigmoid(gates_in[1] + gates_st[1])
    candidate = jnp.tanh(gates_in[2] + reset_gate * gates_st[2])
    old_state = lax.dynamic_slice_in_dim(memory, mp_index * col_share, col_share, 1).astype(
        jnp.float32
    )
    updated = (1.0 - update_gate) * candidate + update_gate * old_state
    new_memory = jnp.where((counts > 0.0)[:, None], updated, old_state).astype(jnp.bfloat16)
    outgoing = jnp.take(new_memory, state_slots, axis=0)
    relayed = lax.all_to_all(outgoing, "nodes", split_axis=0, concat_axis=0, tiled=True)
    relayed = relayed.reshape(relayed.shape[0] * relayed.shape[1], col_share)
    neigh_rows = jnp.take(relayed, neighbours, axis=0).astype(jnp.float32)
    neigh_mean = (jnp.sum(neigh_rows, axis=1) / neighbours.shape[1]).astype(jnp.bfloat16)
    self_state = jnp.take(new_memory, query_slots, axis=0)
    summed = lax.psum_scatter(
        (
            jnp.dot(neigh_mean, w_neigh, preferred_element_type=jnp.float32)
            + jnp.dot(self_state, w_self, preferred_element_type=jnp.float32)
        ).astype(jnp.bfloat16),
        "mp",
        scatter_dimension=0,
        tiled=True,
    ).astype(jnp.float32)
    embedding = jax.nn.relu(summed + b_embed).astype(jnp.bfloat16)
    return (new_memory, embedding)


def solution(mesh):
    in_specs = (
        P("nodes", None),
        P("nodes", None),
        P("nodes"),
        P("nodes", None),
        P(None, "mp"),
        P(None, "mp"),
        P("mp"),
        P("mp", None),
        P(),
        P(None, None, "mp"),
        P(None, None, "mp"),
        P(None, "mp"),
        P(None, "mp"),
        P("nodes", None),
        P("nodes", None),
        P("nodes"),
        P("mp", None),
        P("mp", None),
        P(),
    )
    out_specs = (P("nodes", "mp"), P(("nodes", "mp"), None))
    return jax.shard_map(
        per_device, mesh=mesh, in_specs=in_specs, out_specs=out_specs, check_vma=False
    )
```

profile of v0, /device:TPU:0, one launch (start us, length us, event | category | flops | bytes accessed | tf_op | source)
XLA Modules:
  0.0 198.6 jit_solution(2019015943518735116)
XLA Ops:
  8.0 2.3 %reduce-window.6 = s32[8,8,128]{2,1,0:T(8,128)S(1)} reduce-window(s32[8,8,128]{2,1,0:T(8,128)S(1)} %fusion.38, s32[]{:T(128)} %constant.48.clone.1), window={size=1x1x128 pad=0_0x0_0x127_0}, to_apply=%region_0.0 | reduce-window | flops 1040384 | bytes 65540 | tf_op jit(solution)/shard_map/reduce-window
  12.2 5.0 %scatter_custom_fusion = s32[2048]{0:T(1024)} fusion(s32[1024]{0:T(1024)S(1)} %bitcast.74, s32[1024]{0:T(1024)} %param.21, s32[]{:T(128)} %constant.46.clone.1), kind=kCustom, calls=%fused_computation.83 | custom fusion | bytes 8704 | tf_op jit(solution)/shard_map/scatter | solution.py:44
  17.2 7.3 %all-to-all-start = ((s32[8,1,256]{2,1,0:T(1,128)}), s32[8,1,256]{2,1,0:T(1,128)S(1)}, u32[]{:S(2)}, u32[]{:S(2)}) async-start(s32[8,1,256]{2,1,0:T(1,128)} %bitcast.5), calls=%async_computation | async-start | bytes 16384 | tf_op jit(solution)/shard_map/all_to_all | solution.py:51
  24.5 7.2 %scatter_custom_fusion.2 = bf16[2048,512]{1,0:T(8,128)(2,1)} fusion(s32[1024]{0:T(1024)S(1)} %bitcast.75, bf16[1024,512]{1,0:T(8,128)(2,1)} %param.19, bf16[]{:T(256)} %constant.51.clone.1), kind=kCustom, calls=%fused_computation.21 | custom fusion | bytes 2097664 | tf_op jit(solution)/shard_map/scatter | solution.py:47
  31.7 6.1 %all-to-all-start.1 = ((bf16[8,256,512]{2,1,0:T(8,128)(2,1)}), bf16[8,256,512]{2,1,0:T(8,128)(2,1)}, u32[]{:S(2)}, u32[]{:S(2)}) async-start(bf16[8,256,512]{2,1,0:T(8,128)(2,1)} %bitcast.63), calls=%async_computation.1 | async-start | bytes 4194304 | tf_op jit(solution)/shard_map/all_to_all | solution.py:50
  38.4 1.5 fusion.45
  39.9 2.6 %fusion.4 = f32[3,256,256]{2,1,0:T(8,128)} fusion(bf16[3,1024,256]{2,1,0:T(8,128)(2,1)S(1)} %copy-done, bf16[256,1024]{1,0:T(8,128)(2,1)} %param.22, f32[3,256]{1,0:T(4,128)S(1)} %copy-done.12), kind=kOutput, calls=%fused_computation.17 | convolution fusion | flops 402849792 | bytes 2886656 | tf_op jit(solution)/shard_map/nd,gdc->gnc/dot_general | solution.py:84
  42.5 8.9 %gather_fusion = f32[2048,512]{1,0:T(8,128)} fusion(f32[256,512]{1,0:T(8,128)S(1)} %fusion.45, s32[2048]{0:T(1024)S(1)} %broadcast_clamp_fusion), kind=kCustom, calls=%fused_computation | custom fusion | bytes 8396800 | tf_op jit(solution)/shard_map/jit(_take)/gather | solution.py:61
  51.4 14.7 %scatter_custom_fusion.1 = f32[257]{0:T(512)S(1)} fusion(s32[2048]{0:T(1024)S(1)} %bitcast.72, f32[2048]{0:T(1024)S(1)} %get-tuple-element.2, f32[]{:T(128)} %constant.39.clone.1), kind=kCustom, calls=%fused_computation.88 | custom fusion | flops 2048 | bytes 1032 | tf_op jit(solution)/shard_map/scatter-add | solution.py:73
  66.1 19.6 %all-to-all-done.1 = bf16[8,256,512]{2,1,0:T(8,128)(2,1)} async-done(((bf16[8,256,512]{2,1,0:T(8,128)(2,1)}), bf16[8,256,512]{2,1,0:T(8,128)(2,1)}, u32[]{:S(2)}, u32[]{:S(2)}) %all-to-all-start.1) | async-done | bytes 2097184 | tf_op jit(solution)/shard_map/all_to_all | solution.py:50
  85.6 5.6 %maximum_convert_fusion = bf16[2048,512]{1,0:T(8,128)(2,1)} fusion(f32[2048,512]{1,0:T(8,128)} %gather_fusion, bf16[2048,512]{1,0:T(8,128)(2,1)} %bitcast.10, bf16[512,512]{1,0:T(8,128)(2,1)S(1)} %copy-done.11, f32[512]{0:T(512)S(1)} %copy-done.15, pred[2048]{0:T(1024)(128)(4,1)S(1)} %get-tuple-element.3), kind=kOutput, calls=%fused_computation.11 | convolution fusion | flops 1078984704 | bytes 8916992 | tf_op jit(solution)/shard_map/dot_general | solution.py:60
  91.2 15.1 %scatter_custom_fusion.3 = f32[257,512]{1,0:T(8,128)S(1)} fusion(s32[2048]{0:T(1024)S(1)} %bitcast.73, bf16[2048,512]{1,0:T(8,128)(2,1)} %maximum_convert_fusion, f32[]{:T(128)} %constant.39.clone.1), kind=kCustom, calls=%fused_computation.9 | custom fusion | flops 2097152 | bytes 2623492 | tf_op jit(solution)/shard_map/scatter-add | solution.py:65
  106.8 1.3 fusion.2
  108.1 31.8 %all-reduce.2.cloned.1.call-done = bf16[256,1024]{1,0:T(8,128)(2,1)} async-done(((bf16[256,1024]{1,0:T(8,128)(2,1)}), bf16[256,1024]{1,0:T(8,128)(2,1)}) %all-reduce.2.cloned.1.call-update) | async-done | bytes 524304 | tf_op jit(solution)/shard_map/psum | solution.py:77
  139.9 2.2 %fusion.5 = f32[3,256,256]{2,1,0:T(8,128)S(1)} fusion(bf16[3,1024,256]{2,1,0:T(8,128)(2,1)} %param.28, bf16[256,1024]{1,0:T(8,128)(2,1)} %all-reduce.2.cloned.1.call-done, f32[1024]{0:T(1024)S(1)} %copy-done.13, f32[256]{0:T(256)S(1)} %slice_maximum_fusion, f32[3,256]{1,0:T(4,128)S(1)} %copy-done.14), kind=kOutput, calls=%fused_computation.19 | convolution fusion | flops 403898368 | bytes 2891776 | tf_op jit(solution)/shard_map/nd,gdc->gnc/dot_general | solution.py:80
  143.3 1.2 gather_fusion.1
  145.2 5.5 %all-to-all-start.2 = ((bf16[8,32,256]{2,1,0:T(8,128)(2,1)}), bf16[8,32,256]{2,1,0:T(8,128)(2,1)S(1)}, u32[]{:S(2)}, u32[]{:S(2)}) async-start(bf16[8,32,256]{2,1,0:T(8,128)(2,1)} %broadcast_select_fusion), calls=%async_computation.2 | async-start | bytes 262144 | tf_op jit(solution)/shard_map/all_to_all | solution.py:96
  150.9 1.2 gather_fusion.3
  152.1 6.0 %all-to-all-done.2 = bf16[8,32,256]{2,1,0:T(8,128)(2,1)S(1)} async-done(((bf16[8,32,256]{2,1,0:T(8,128)(2,1)}), bf16[8,32,256]{2,1,0:T(8,128)(2,1)S(1)}, u32[]{:S(2)}, u32[]{:S(2)}) %all-to-all-start.2) | async-done | bytes 131104 | tf_op jit(solution)/shard_map/all_to_all | solution.py:96
  158.0 7.6 %gather_fusion.2 = bf16[2560,256]{1,0:T(8,128)(2,1)S(1)} fusion(bf16[256,256]{1,0:T(8,128)(2,1)S(1)} %bitcast.62, s32[3072]{0:T(1024)S(1)} %pad_clamp_fusion), kind=kCustom, calls=%fused_computation.2 | custom fusion | bytes 2631680 | tf_op jit(solution)/shard_map/jit(_take)/gather | solution.py:98
  165.6 1.6 reshape.152
  167.2 2.8 %convert_reduce_fusion = f32[256,256]{1,0:T(8,128)S(1)} fusion(bf16[256,10,256]{2,1,0:T(8,128)(2,1)} %reshape.152, pred[256,10]{1,0:T(8,128)(4,1)S(1)} %copy.26), kind=kLoop, calls=%fused_computation.8 | loop fusion | flops 1900544 | bytes 1575424 | tf_op jit(solution)/shard_map/reduce_sum | solution.py:99
  171.5 18.7 %reduce-scatter.2.cloned.1.call-done = bf16[64,1024]{1,0:T(8,128)(2,1)} async-done(((bf16[256,1024]{1,0:T(8,128)(2,1)}), bf16[64,1024]{1,0:T(8,128)(2,1)}) %reduce-scatter.2.cloned.1.call-update) | async-done | bytes 131088 | tf_op jit(solution)/shard_map/reduce_scatter | solution.py:101
  190.2 1.6 maximum_convert_fusion.1
  (66 shorter events, 7.3 us)
Async XLA Ops:
  7.2 32.7 %copy-start = (bf16[3,1024,256]{2,1,0:T(8,128)(2,1)S(1)}, bf16[3,1024,256]{2,1,0:T(8,128)(2,1)}, u32[]{:S(2)}) copy-start(bf16[3,1024,256]{2,1,0:T(8,128)(2,1)} %param.29) | copy-start | bytes 4718596
  17.2 14.5 %all-to-all-start = ((s32[8,1,256]{2,1,0:T(1,128)}), s32[8,1,256]{2,1,0:T(1,128)S(1)}, u32[]{:S(2)}, u32[]{:S(2)}) async-start(s32[8,1,256]{2,1,0:T(1,128)} %bitcast.5), calls=%async_computation | async-start | bytes 16384 | tf_op jit(solution)/shard_map/all_to_all | solution.py:51
  31.7 6.2 %copy-start.8 = (s32[8,32]{1,0:T(8,128)S(1)}, s32[8,32]{1,0:T(8,128)}, u32[]{:S(2)}) copy-start(s32[8,32]{1,0:T(8,128)} %param.32) | copy-start | bytes 3076
  31.7 6.3 %copy-start.7 = (s32[256,10]{0,1:T(8,128)S(1)}, s32[256,10]{0,1:T(8,128)}, u32[]{:S(2)}) copy-start(s32[256,10]{0,1:T(8,128)} %param.33) | copy-start | bytes 30724
  31.7 6.6 %copy-start.10 = (s32[256]{0:T(256)S(1)}, s32[256]{0:T(256)}, u32[]{:S(2)}) copy-start(s32[256]{0:T(256)} %param.34) | copy-start | bytes 3076
  31.7 6.7 %copy-start.3 = (bf16[1024,512]{1,0:T(8,128)(2,1)S(1)}, bf16[1024,512]{1,0:T(8,128)(2,1)}, u32[]{:S(2)}) copy-start(bf16[1024,512]{1,0:T(8,128)(2,1)} %param.24) | copy-start | bytes 3145732
  31.7 53.9 %all-to-all-start.1 = ((bf16[8,256,512]{2,1,0:T(8,128)(2,1)}), bf16[8,256,512]{2,1,0:T(8,128)(2,1)}, u32[]{:S(2)}, u32[]{:S(2)}) async-start(bf16[8,256,512]{2,1,0:T(8,128)(2,1)} %bitcast.63), calls=%async_computation.1 | async-start | bytes 4194304 | tf_op jit(solution)/shard_map/all_to_all | solution.py:50
  37.9 2.0 %copy-start.12 = (f32[3,256]{1,0:T(4,128)S(1)}, f32[3,256]{1,0:T(4,128)}, u32[]{:S(2)}) copy-start(f32[3,256]{1,0:T(4,128)} %param.31) | copy-start | bytes 9220
  37.9 102.0 %all-reduce.2.cloned.1.call-start = ((), (), s32[]{:S(2)}) async-start(), calls=%async_computation.4 | async-start | bytes 1048576 | tf_op jit(solution)/shard_map/psum | solution.py:77
  42.5 43.2 %copy-start.11 = (bf16[512,512]{1,0:T(8,128)(2,1)S(1)}, bf16[512,512]{1,0:T(8,128)(2,1)}, u32[]{:S(2)}) copy-start(bf16[512,512]{1,0:T(8,128)(2,1)} %param.23) | copy-start | bytes 1572868
  42.5 43.2 %copy-start.15 = (f32[512]{0:T(512)S(1)}, f32[512]{0:T(512)}, u32[]{:S(2)}) copy-start(f32[512]{0:T(512)} %param.25) | copy-start | bytes 6148
  91.2 15.1 %copy-start.2 = (bf16[512,1024]{1,0:T(8,128)(2,1)S(1)}, bf16[512,1024]{1,0:T(8,128)(2,1)}, u32[]{:S(2)}) copy-start(bf16[512,1024]{1,0:T(8,128)(2,1)} %param.26) | copy-start | bytes 3145732
  106.8 33.1 %copy-start.13 = (f32[1024]{0:T(1024)S(1)}, f32[1024]{0:T(1024)}, u32[]{:S(2)}) copy-start(f32[1024]{0:T(1024)} %param.27) | copy-start | bytes 12292
  106.8 33.1 %copy-start.14 = (f32[3,256]{1,0:T(4,128)S(1)}, f32[3,256]{1,0:T(4,128)}, u32[]{:S(2)}) copy-start(f32[3,256]{1,0:T(4,128)} %param.30) | copy-start | bytes 9220
  108.1 34.0 %copy-start.4 = (f32[3,256,256]{2,1,0:T(8,128)S(1)}, f32[3,256,256]{2,1,0:T(8,128)}, u32[]{:S(2)}) copy-start(f32[3,256,256]{2,1,0:T(8,128)} %fusion.4) | copy-start | bytes 2359300
  143.3 22.4 %copy-start.1 = (bf16[256,256]{1,0:T(8,128)(2,1)}, bf16[256,256]{1,0:T(8,128)(2,1)S(1)}, u32[]{:S(2)}) copy-start(bf16[256,256]{1,0:T(8,128)(2,1)S(1)} %fusion.15) | copy-start | bytes 393220
  145.2 12.9 %all-to-all-start.2 = ((bf16[8,32,256]{2,1,0:T(8,128)(2,1)}), bf16[8,32,256]{2,1,0:T(8,128)(2,1)S(1)}, u32[]{:S(2)}, u32[]{:S(2)}) async-start(bf16[8,32,256]{2,1,0:T(8,128)(2,1)} %broadcast_select_fusion), calls=%async_computation.2 | async-start | bytes 262144 | tf_op jit(solution)/shard_map/all_to_all | solution.py:96
  150.7 39.5 %reduce-scatter.2.cloned.1.call-start = ((), (), s32[]{:S(2)}) async-start(), calls=%async_computation.5 | async-start | bytes 655360 | tf_op jit(solution)/shard_map/reduce_scatter | solution.py:101
  167.2 2.8 %copy-start.5 = (bf16[256,1024]{1,0:T(8,128)(2,1)S(1)}, bf16[256,1024]{1,0:T(8,128)(2,1)}, u32[]{:S(2)}) copy-start(bf16[256,1024]{1,0:T(8,128)(2,1)} %param.35) | copy-start | bytes 1572868
  167.2 3.1 %copy-start.6 = (bf16[256,1024]{1,0:T(8,128)(2,1)S(1)}, bf16[256,1024]{1,0:T(8,128)(2,1)}, u32[]{:S(2)}) copy-start(bf16[256,1024]{1,0:T(8,128)(2,1)} %param.36) | copy-start | bytes 1572868
  170.0 20.2 %copy-start.9 = (f32[1024]{0:T(1024)S(1)}, f32[1024]{0:T(1024)}, u32[]{:S(2)}) copy-start(f32[1024]{0:T(1024)} %param.37) | copy-start | bytes 12292
Sparse Core Ops, SparseCore 0:
  108.2 31.6 all-reduce.1
  171.6 18.4 reduce-scatter.1
where the time goes:
time: 200 us; the launch traced here: 199 us
  waiting for transfers between devices  76 us (38%)
  other arithmetic  40.8 us (20%)
  local copies, waits for them, and re-layouts  33.4 us (17%)
  starting transfers between devices  19 us (10%)
  matrix products  15 us (8%)
  between operations  14.4 us (7%)
    psum x1, waiting for transfers between devices, per_device(): lax.psum(partial_total.astype(jnp.bfloat16), 'mp').astype(jnp.float32)  31.8 us
    all_to_all x1, waiting for transfers between devices, per_device(): lax.all_to_all(feat_buffer, 'nodes', split_axis=0, concat_axis=0, tiled=T...  19.6 us
    reduce_scatter x1, waiting for transfers between devices, per_device(): lax.psum_scatter((jnp.dot(neigh_mean, w_neigh, preferred_element_type=jnp...  18.7 us
    scatter-add x1, other arithmetic, per_device(): jax.ops.segment_sum(hidden_msg.astype(jnp.float32), segment_ids, num_segm...  15.1 us
    scatter-add x1, other arithmetic, per_device(): jax.ops.segment_sum(valid.astype(jnp.float32), segment_ids, num_segments=...  14.7 us
    gather x2, local copies, waits for them, and re-layouts, per_device(): neigh_rows = jnp.take(relayed, neighbours, axis=0).astype(jnp.float32)  9.14 us
    gather x1, local copies, waits for them, and re-layouts, per_device(): jnp.take(state_proj, safe_ids, axis=0)  8.91 us
    all_to_all x1, starting transfers between devices, per_device(): lax.all_to_all(id_buffer, 'nodes', split_axis=0, concat_axis=0, tiled=True)  7.28 us
  transfers between devices with their start and end apart: 5, of which 4 were waited for; matrix products, arithmetic and copies ran while one was open for 18% of the time, Pallas kernels for 0%

commit v1 on v0

v1 whole, which is shorter than its diff:
```python
import functools

import jax
import jax.numpy as jnp
from jax import lax
from jax.experimental import pallas as pl
from jax.experimental.pallas import tpu as pltpu
from jax.sharding import PartitionSpec as P

BF = jnp.bfloat16
F32 = jnp.float32
MESH = pl.DeviceIdType.MESH
LANES = 128


def iota(shape, dim):
    return lax.broadcasted_iota(jnp.int32, shape, dim)


def fiota(shape, dim):
    return iota(shape, dim).astype(F32)


def ones_where(cond):
    return jnp.where(cond, 1.0, 0.0)


def to_col(row):
    size = row.shape[1]
    eye = iota((size, size), 0) == iota((size, size), 1)
    return jnp.sum(jnp.where(eye, row, 0.0), axis=1, keepdims=True)


def to_row(col):
    size = col.shape[0]
    eye = iota((size, size), 0) == iota((size, size), 1)
    return jnp.sum(jnp.where(eye, col, 0.0), axis=0, keepdims=True)


def dot(a, b):
    return jnp.dot(a, b, preferred_element_type=F32)


def kernel(
    n,
    owner_ref, slot_ref, b_msg_ref, b_out_ref, b_in_ref, b_hid_ref,
    sslots_ref, neigh_ref, query_ref, b_emb_ref,
    feats_hbm, mem_hbm, wev_hbm, wst_hbm, wout_hbm, win_hbm, whid_hbm, wn_hbm, ws_hbm,
    new_ref, emb_ref,
    feats, mem, wev, wst, wout, win, whid, wn, ws,
    target, slotcol, send_buf, ids_send, arr, ids, proj_hi, proj_lo, gst,
    acc, cnt, ar_s1, ar_r1, p_own, ar_s2, ar_r2, agg_own, agg_oth,
    smat, cmat, qmat, newm, st_send, st_recv, selfp, rs_send, rs_recv,
    load_sem, ds_sem, dr_sem, is_sem, ir_sem, xs_sem, xr_sem,
    c1s_sem, c1r_sem, c2s_sem, c2r_sem, ar_ssem, ar_rsem, ss_sem, sr_sem, rs_ssem, rs_rsem,
):
    me = lax.axis_index("nodes")
    m = lax.axis_index("mp")
    core = m + 1 - 2 * (m % 2)
    cross = (m + 2) % 4
    far = (core + 2) % 4
    events = owner_ref.shape[1]
    cap = send_buf.shape[1]
    nodes = mem.shape[0]
    width = mem.shape[1]
    share = width // 4
    half = width // 2
    scap = sslots_ref.shape[1]
    qblock = emb_ref.shape[0]
    fcols = feats.shape[1]

    loads = []

    def load(src, dst):
        c = pltpu.make_async_copy(src, dst, load_sem.at[len(loads)])
        c.start()
        loads.append(c)
        return c

    ld_feats = load(feats_hbm.at[:, pl.ds(pl.multiple_of(m * fcols, fcols), fcols)], feats)
    ld_mem = load(mem_hbm, mem)
    ld_wst = load(wst_hbm, wst)
    ld_wev = load(wev_hbm, wev)
    ld_whid = load(whid_hbm, whid)
    ld_wout = load(wout_hbm, wout)
    ld_win = load(win_hbm, win)
    ld_ws = load(ws_hbm, ws)
    ld_wn = load(wn_hbm, wn)

    barrier = pltpu.get_barrier_semaphore()

    def greet(k, c):
        pl.semaphore_signal(barrier, inc=1, device_id=((me + k) % n, m), device_id_type=MESH)
        return c

    lax.fori_loop(1, n, greet, 0)
    pl.semaphore_signal(barrier, inc=1, device_id=(me, core), device_id_type=MESH)
    pl.semaphore_signal(barrier, inc=1, device_id=(me, cross), device_id_type=MESH)

    rows = max(n, 16)
    oi = iota((rows, LANES), 0)
    tri = ones_where(iota((LANES, LANES), 0) < iota((LANES, LANES), 1)).astype(BF)
    running = jnp.zeros((rows, 1), F32)
    for j in range(events // LANES):
        at = slice(j * LANES, (j + 1) * LANES)
        ow = owner_ref[:, at]
        match = ones_where(ow == oi)
        before = dot(match.astype(BF), tri) + running
        place = jnp.sum(match * before, axis=0, keepdims=True)
        target[:, at] = ow.astype(F32) * float(cap) + place
        running = running + jnp.sum(match, axis=1, keepdims=True)
        col = to_col(slot_ref[:, at].astype(F32) + 1.0)
        slotcol[at, :] = jnp.broadcast_to(col, (LANES, LANES)).astype(BF)

    pl.semaphore_wait(barrier, n + 1)
    ld_feats.wait()

    def dispatch_copies(d, s):
        return (
            pltpu.make_async_remote_copy(
                src_ref=send_buf.at[d], dst_ref=arr.at[m, s],
                send_sem=ds_sem.at[d], recv_sem=dr_sem.at[s],
                device_id=(d, m), device_id_type=MESH,
            ),
            pltpu.make_async_remote_copy(
                src_ref=ids_send.at[d], dst_ref=ids.at[s],
                send_sem=is_sem.at[d], recv_sem=ir_sem.at[s],
                device_id=(d, m), device_id_type=MESH,
            ),
        )

    def dispatch(k, c):
        d = (me + k) % n
        pick = ones_where(
            target[...] == fiota((cap, events), 0) + (d * cap).astype(F32)
        ).astype(BF)
        out = dot(pick, jnp.concatenate([feats[...], slotcol[...]], axis=1))
        block = out[:, :fcols].astype(BF)
        idrow = jnp.broadcast_to(to_row(out[:, fcols:fcols + 1]), (8, cap))

        @pl.when(k < n)
        def _():
            send_buf[d] = block
            ids_send[d] = idrow
            for cp in dispatch_copies(d, me):
                cp.start()

        @pl.when(k == n)
        def _():
            arr[m, me] = block
            ids[me] = idrow

        return c

    lax.fori_loop(1, n + 1, dispatch, 0)

    ld_mem.wait()
    ld_wst.wait()
    proj = dot(mem[...], wst[...]) + b_msg_ref[...]
    hi = proj.astype(BF)
    proj_hi[...] = hi
    proj_lo[...] = (proj - hi.astype(F32)).astype(BF)
    acc[...] = jnp.zeros_like(acc)
    cnt[...] = jnp.zeros_like(cnt)
    ld_wev.wait()

    def relay(src_col, s, to, ssem, rsem):
        return pltpu.make_async_remote_copy(
            src_ref=arr.at[src_col, s], dst_ref=arr.at[src_col, s],
            send_sem=ssem.at[s], recv_sem=rsem.at[s],
            device_id=(me, to), device_id_type=MESH,
        )

    def step(i, c):
        @pl.when(i < n)
        def _():
            s = (me - i + n) % n

            @pl.when(i > 0)
            def _():
                for cp in dispatch_copies(s, s):
                    cp.wait_recv()

            relay(m, s, cross, xs_sem, xr_sem).start()
            relay(m, s, core, c1s_sem, c1r_sem).start()

        @pl.when(jnp.logical_and(i >= 1, i <= n))
        def _():
            s = (me - i + 1 + n) % n
            relay(cross, s, cross, xs_sem, xr_sem).wait_recv()
            relay(cross, s, core, c2s_sem, c2r_sem).start()

        @pl.when(i >= 2)
        def _():
            s = (me - i + 2 + n) % n
            relay(core, s, core, c1s_sem, c1r_sem).wait_recv()
            relay(far, s, core, c2s_sem, c2r_sem).wait_recv()
            x = jnp.concatenate([arr[j, s] for j in range(4)], axis=1)
            row = ids[s][0:1, :]
            oh = ones_where(to_col(row) == fiota((cap, nodes), 1) + 1.0).astype(BF)
            oht = ones_where(row == fiota((nodes, cap), 0) + 1.0)
            pre = dot(x, wev[...]) + dot(oh, proj_hi[...]) + dot(oh, proj_lo[...])
            hidden = jnp.maximum(pre, 0.0).astype(BF)
            acc[...] += dot(oht.astype(BF), hidden)
            cnt[...] += jnp.sum(oht, axis=1, keepdims=True)

        @pl.when(i == 0)
        def _():
            for g in range(3):
                gst[g] = dot(mem[...], whid[g]) + b_hid_ref[g:g + 1, :]

        @pl.when(i == 1)
        def _():
            lane = iota((qmat.shape[0], cmat.shape[1]), 1)
            total = jnp.zeros(cmat.shape, F32)
            for k in range(neigh_ref.shape[1]):
                total = total + ones_where(neigh_ref[:, k:k + 1] == lane)
            cmat[...] = total.astype(BF)
            qcol = to_col(query_ref[...].astype(F32))
            qmat[...] = ones_where(qcol == fiota(qmat.shape, 1)).astype(BF)

            def fill(d, c):
                col = to_col(sslots_ref[pl.ds(d, 1), :].astype(F32))
                smat[pl.ds(pl.multiple_of(d * scap, scap), scap), :] = ones_where(
                    col == fiota((scap, nodes), 1)
                ).astype(BF)
                return c

            lax.fori_loop(0, n, fill, 0)

        return c

    ld_whid.wait()
    lax.fori_loop(0, n + 2, step, 0)

    ld_wout.wait()
    chunks = 2
    crows = nodes // chunks
    my_half = pl.ds(pl.multiple_of((m % 2) * half, half), half)
    its_half = pl.ds(pl.multiple_of((core % 2) * half, half), half)

    def ar_copy(stage, r, src, dst, to):
        at = pl.ds(r * crows, crows)
        return pltpu.make_async_remote_copy(
            src_ref=src.at[at, :], dst_ref=dst.at[at, :],
            send_sem=ar_ssem.at[stage * chunks + r], recv_sem=ar_rsem.at[stage * chunks + r],
            device_id=(me, to), device_id_type=MESH,
        )

    def sum_out(r, cols):
        at = pl.ds(r * crows, crows)
        a = acc[at, :]
        head = a.astype(BF)
        tail = (a - head.astype(F32)).astype(BF)
        w = wout[:, cols]
        return dot(head, w) + dot(tail, w)

    stage1 = [ar_copy(0, r, ar_s1, ar_r1, core) for r in range(chunks)]
    stage2 = [ar_copy(1, r, ar_s2, ar_r2, cross) for r in range(chunks)]
    stage3 = [ar_copy(2, r, agg_own, agg_oth, core) for r in range(chunks)]
    for r in range(chunks):
        at = pl.ds(r * crows, crows)
        ar_s1[at, :] = sum_out(r, its_half).astype(BF)
        stage1[r].start()
    for r in range(chunks):
        at = pl.ds(r * crows, crows)
        own = sum_out(r, my_half)
        stage1[r].wait_recv()
        own = own + ar_r1[at, :].astype(F32)
        p_own[at, :] = own
        ar_s2[at, :] = own.astype(BF)
        stage2[r].start()
    ld_win.wait()
    for r in range(chunks):
        at = pl.ds(r * crows, crows)
        stage2[r].wait_recv()
        total = p_own[at, :] + ar_r2[at, :].astype(F32)
        agg = total / jnp.maximum(cnt[at, :][:, 0:1], 1.0) + b_out_ref[:, my_half]
        agg_own[at, :] = agg.astype(BF)
        stage3[r].start()
    for r in range(chunks):
        at = pl.ds(r * crows, crows)
        mine = [dot(agg_own[at, :], win[g, my_half, :]) for g in range(3)]
        stage3[r].wait_recv()
        gin = [
            mine[g] + dot(agg_oth[at, :], win[g, its_half, :]) + b_in_ref[g:g + 1, :]
            for g in range(3)
        ]
        reset = jax.nn.sigmoid(gin[0] + gst[0, at, :])
        update = jax.nn.sigmoid(gin[1] + gst[1, at, :])
        cand = jnp.tanh(gin[2] + reset * gst[2, at, :])
        old = mem[at, pl.ds(pl.multiple_of(m * share, share), share)].astype(F32)
        upd = (1.0 - update) * cand + update * old
        out = jnp.where(cnt[at, :][:, 0:1] > 0.0, upd, old).astype(BF)
        newm[at, :] = out
        new_ref[at, :] = out

    def state_copy(d, s):
        return pltpu.make_async_remote_copy(
            src_ref=st_send.at[pl.ds(pl.multiple_of(d * scap, scap), scap), :],
            dst_ref=st_recv.at[pl.ds(pl.multiple_of(s * scap, scap), scap), :],
            send_sem=ss_sem.at[d], recv_sem=sr_sem.at[s],
            device_id=(d, m), device_id_type=MESH,
        )

    st_send[...] = dot(smat[...], newm[...]).astype(BF)

    def send_state(k, c):
        state_copy((me + k) % n, me).start()
        return c

    lax.fori_loop(1, n, send_state, 0)
    mine = pl.ds(pl.multiple_of(me * scap, scap), scap)
    st_recv[mine, :] = st_send[mine, :]
    ld_ws.wait()
    selfp[...] = dot(dot(qmat[...], newm[...]).astype(BF), ws[...])
    ld_wn.wait()

    def recv_state(k, c):
        s = (me - k + n) % n
        state_copy(s, s).wait_recv()
        return c

    lax.fori_loop(1, n, recv_state, 0)

    def rs_copy(j, to):
        return pltpu.make_async_remote_copy(
            src_ref=rs_send.at[j], dst_ref=rs_recv.at[j],
            send_sem=rs_ssem.at[j], recv_sem=rs_rsem.at[j],
            device_id=(me, to), device_id_type=MESH,
        )

    def embed(b):
        at = pl.ds(pl.multiple_of(b * qblock, qblock), qblock)
        mean = (dot(cmat[at, :], st_recv[...]) / float(neigh_ref.shape[1])).astype(BF)
        return dot(mean, wn[...]) + selfp[at, :]

    to_core = [rs_copy(0, core), rs_copy(1, core)]
    to_cross = rs_copy(2, cross)
    rs_send[0] = embed(far).astype(BF)
    to_core[0].start()
    rs_send[1] = embed(core).astype(BF)
    to_core[1].start()
    part = embed(cross)
    to_core[0].wait_recv()
    rs_send[2] = (part + rs_recv[0].astype(F32)).astype(BF)
    to_cross.start()
    part = embed(m)
    to_core[1].wait_recv()
    part = part + rs_recv[1].astype(F32) + b_emb_ref[...]
    to_cross.wait_recv()
    emb_ref[...] = jnp.maximum(part + rs_recv[2].astype(F32), 0.0).astype(BF)

    def drain(s, c):
        relay(m, s, cross, xs_sem, xr_sem).wait_send()
        relay(m, s, core, c1s_sem, c1r_sem).wait_send()
        relay(cross, s, core, c2s_sem, c2r_sem).wait_send()
        return c

    lax.fori_loop(0, n, drain, 0)

    def drain_peers(k, c):
        d = (me + k) % n
        for cp in dispatch_copies(d, me):
            cp.wait_send()
        state_copy(d, me).wait_send()
        return c

    lax.fori_loop(1, n, drain_peers, 0)
    for cp in stage1 + stage2 + stage3 + to_core + [to_cross]:
        cp.wait_send()


def per_device(
    event_feats, event_owner, event_slot, memory, w_msg_event, w_msg_state, b_msg, w_msg_out,
    b_out, w_input, w_hidden, b_input, b_hidden, state_slots, neighbours, query_slots,
    w_neigh, w_self, b_embed,
):
    n = lax.axis_size("nodes")
    shares = lax.axis_size("mp")
    assert shares == 4
    events, feat = event_feats.shape
    nodes, width = memory.shape
    cap = 2 * events // n
    share = width // shares
    hid = w_msg_event.shape[1]
    half = width // 2
    scap = state_slots.shape[1]
    queries = query_slots.shape[0]
    qblock = queries // shares
    fcols = feat // shares
    vm = pl.BlockSpec(memory_space=pltpu.VMEM)
    hbm = pl.BlockSpec(memory_space=pl.ANY)
    V = pltpu.VMEM
    dma = lambda k: pltpu.SemaphoreType.DMA((k,))
    scratch = [
        V((events, fcols), BF), V(memory.shape, BF), V(w_msg_event.shape, BF),
        V(w_msg_state.shape, BF), V(w_msg_out.shape, BF), V(w_input.shape, BF),
        V(w_hidden.shape, BF), V(w_neigh.shape, BF), V(w_self.shape, BF),
        V((1, events), F32), V((events, LANES), BF), V((n, cap, fcols), BF),
        V((n, 8, cap), F32), V((4, n, cap, fcols), BF), V((n, 8, cap), F32),
        V((nodes, hid), BF), V((nodes, hid), BF), V((3, nodes, share), F32),
        V((nodes, hid), F32), V((nodes, LANES), F32),
        V((nodes, half), BF), V((nodes, half), BF), V((nodes, half), F32),
        V((nodes, half), BF), V((nodes, half), BF), V((nodes, half), BF), V((nodes, half), BF),
        V((n * scap, nodes), BF), V((queries, n * scap), BF), V((queries, nodes), BF),
        V((nodes, share), BF), V((n * scap, share), BF), V((n * scap, share), BF),
        V((queries, width), F32), V((3, qblock, width), BF), V((3, qblock, width), BF),
        dma(9), dma(n), dma(n), dma(n), dma(n), dma(n), dma(n),
        dma(n), dma(n), dma(n), dma(n), dma(6), dma(6), dma(n), dma(n), dma(3), dma(3),
    ]
    return pl.pallas_call(
        functools.partial(kernel, n),
        out_shape=(
            jax.ShapeDtypeStruct((nodes, share), BF),
            jax.ShapeDtypeStruct((qblock, width), BF),
        ),
        in_specs=[vm] * 10 + [hbm] * 9,
        out_specs=(vm, vm),
        scratch_shapes=scratch,
        compiler_params=pltpu.CompilerParams(
            collective_id=0, has_side_effects=True, vmem_limit_bytes=40 * 1024 * 1024
        ),
        cost_estimate=pl.CostEstimate(flops=8_000_000_000, bytes_accessed=9_000_000, transcendentals=0),
    )(
        event_owner.reshape(1, events), event_slot.reshape(1, events), b_msg.reshape(1, -1),
        b_out.reshape(1, -1), b_input, b_hidden, state_slots, neighbours,
        query_slots.reshape(1, -1), b_embed.reshape(1, -1),
        event_feats, memory, w_msg_event, w_msg_state, w_msg_out, w_input, w_hidden,
        w_neigh, w_self,
    )


def solution(mesh):
    in_specs = (
        P("nodes", None),
        P("nodes", None),
        P("nodes"),
        P("nodes", None),
        P(None, "mp"),
        P(None, "mp"),
        P("mp"),
        P("mp", None),
        P(),
        P(None, None, "mp"),
        P(None, None, "mp"),
        P(None, "mp"),
        P(None, "mp"),
        P("nodes", None),
        P("nodes", None),
        P("nodes"),
        P("mp", None),
        P("mp", None),
        P(),
    )
    out_specs = (P("nodes", "mp"), P(("nodes", "mp"), None))
    return jax.shard_map(
        per_device, mesh=mesh, in_specs=in_specs, out_specs=out_specs, check_vma=False
    )
```

time: 200 us -> 75.9 us (0.38)
  waiting for transfers between devices: 76 us -> 0 us
  Pallas kernels: 0 us -> 55.4 us
  other arithmetic: 40.8 us -> 0 us
  starting transfers between devices: 19 us -> 0 us
  matrix products: 15 us -> 0 us
  local copies, waits for them, and re-layouts: 33.4 us -> 19 us
  between operations: 14.4 us -> 0.66 us
    pallas_call x0 -> x1, Pallas kernels: none -> 55.4 us  [per_device(): pl.pallas_call(functools.partial(kernel, n), out_shape=(jax.ShapeDtypeStr...]
    psum x1 -> x0, waiting for transfers between devices: 31.8 us -> none  [per_device(): lax.psum(partial_total.astype(jnp.bfloat16), 'mp').astype(jnp.float32)]
    scatter-add x2 -> x0, other arithmetic: 29.8 us -> none  [the longest x1 15.1 us: per_device(): jax.ops.segment_sum(hidden_msg.astype(jnp.float32), segment_ids, num_segm...]
    all_to_all x3 -> x0, waiting for transfers between devices: 25.5 us -> none  [the longest x1 19.6 us: per_device(): lax.all_to_all(feat_buffer, 'nodes', split_axis=0, concat_axis=0, tiled=T...]
    gather x5 -> x0, local copies, waits for them, and re-layouts: 20.4 us -> none  [the longest x2 9.14 us: per_device(): neigh_rows = jnp.take(relayed, neighbours, axis=0).astype(jnp.float32)]
    all_to_all x3 -> x0, starting transfers between devices: 18.9 us -> none  [the longest x1 7.28 us: per_device(): lax.all_to_all(id_buffer, 'nodes', split_axis=0, concat_axis=0, tiled=True)]
    unnamed x32 -> x39, local copies, waits for them, and re-layouts: 0.08 us -> 19 us
    reduce_scatter x1 -> x0, waiting for transfers between devices: 18.7 us -> none  [per_device(): lax.psum_scatter((jnp.dot(neigh_mean, w_neigh, preferred_element_type=jnp...]
  transfers between devices with their start and end apart: 5 -> 0, of which waited for: 4 -> 0; matrix products, arithmetic and copies ran while one was open for 18% -> 0% of each run, Pallas kernels for 0% -> 0%
where the time goes in v1:
time: 75.9 us; the launch traced here: 75.1 us
  Pallas kernels  55.4 us (73%)
  local copies, waits for them, and re-layouts  19 us (25%)
    pallas_call x1, Pallas kernels, per_device(): pl.pallas_call(functools.partial(kernel, n), out_shape=(jax.ShapeDtypeStr...  55.4 us
    unnamed x39, local copies, waits for them, and re-layouts  19 us

profile of v1, /device:TPU:0, one launch (start us, length us, event | category | flops | bytes accessed | tf_op | source)
XLA Modules:
  0.0 75.1 jit_solution(15794594597569892790)
XLA Ops:
  0.6 0.8 %copy.21.neigh_ref = s32[256,10]{1,0:T(8,128)S(1)} copy(s32[256,10]{0,1:T(8,128)} %param.33) | data formatting | bytes 20480 | tf_op args[14]
  1.5 0.0 copy-start
  1.5 1.4 %copy-done = bf16[3,1024,256]{2,1,0:T(8,128)(2,1)S(1)} copy-done((bf16[3,1024,256]{2,1,0:T(8,128)(2,1)S(1)}, bf16[3,1024,256]{2,1,0:T(8,128)(2,1)}, u32[]{:S(2)}) %copy-start) | copy-done | bytes 1572888
  2.9 0.0 copy-start.1
  2.9 1.4 %copy-done.1 = bf16[3,1024,256]{2,1,0:T(8,128)(2,1)S(1)} copy-done((bf16[3,1024,256]{2,1,0:T(8,128)(2,1)S(1)}, bf16[3,1024,256]{2,1,0:T(8,128)(2,1)}, u32[]{:S(2)}) %copy-start.1) | copy-done | bytes 1572888
  4.3 1.2 %copy-done.2 = bf16[1024,512]{1,0:T(8,128)(2,1)S(1)} copy-done((bf16[1024,512]{1,0:T(8,128)(2,1)S(1)}, bf16[1024,512]{1,0:T(8,128)(2,1)}, u32[]{:S(2)}) %copy-start.2) | copy-done | bytes 1048600
  5.5 1.2 %copy-done.3 = bf16[1024,512]{1,0:T(8,128)(2,1)S(1)} copy-done((bf16[1024,512]{1,0:T(8,128)(2,1)S(1)}, bf16[1024,512]{1,0:T(8,128)(2,1)}, u32[]{:S(2)}) %copy-start.3) | copy-done | bytes 1048600
  6.7 1.2 %copy-done.4 = bf16[512,1024]{1,0:T(8,128)(2,1)S(1)} copy-done((bf16[512,1024]{1,0:T(8,128)(2,1)S(1)}, bf16[512,1024]{1,0:T(8,128)(2,1)}, u32[]{:S(2)}) %copy-start.4) | copy-done | bytes 1048600
  8.0 1.0 %copy-done.5 = bf16[256,1024]{1,0:T(8,128)(2,1)S(1)} copy-done((bf16[256,1024]{1,0:T(8,128)(2,1)S(1)}, bf16[256,1024]{1,0:T(8,128)(2,1)}, u32[]{:S(2)}) %copy-start.5) | copy-done | bytes 524312
  9.0 1.0 %copy-done.6 = bf16[512,512]{1,0:T(8,128)(2,1)S(1)} copy-done((bf16[512,512]{1,0:T(8,128)(2,1)S(1)}, bf16[512,512]{1,0:T(8,128)(2,1)}, u32[]{:S(2)}) %copy-start.6) | copy-done | bytes 524312
  10.0 1.0 %copy-done.7 = bf16[256,1024]{1,0:T(8,128)(2,1)S(1)} copy-done((bf16[256,1024]{1,0:T(8,128)(2,1)S(1)}, bf16[256,1024]{1,0:T(8,128)(2,1)}, u32[]{:S(2)}) %copy-start.7) | copy-done | bytes 524312
  11.1 1.0 %copy-done.8 = bf16[256,1024]{1,0:T(8,128)(2,1)S(1)} copy-done((bf16[256,1024]{1,0:T(8,128)(2,1)S(1)}, bf16[256,1024]{1,0:T(8,128)(2,1)}, u32[]{:S(2)}) %copy-start.8) | copy-done | bytes 524312
  12.1 0.7 copy-done.9
  12.8 0.7 copy-done.10
  13.5 0.7 copy-done.11
  14.2 0.7 copy-done.12
  14.9 0.7 copy-done.13
  15.6 0.7 copy-done.14
  16.2 0.7 copy-done.15
  16.9 0.7 copy-done.16
  17.6 0.7 copy-done.17
  18.3 55.4 %shard_map.194 = (bf16[256,256]{1,0:T(8,128)(2,1)S(1)}, bf16[64,1024]{1,0:T(8,128)(2,1)S(1)}) custom-call(s32[1,1024]{1,0:T(1,128)S(1)} %bitcast.6, s32[1,1024]{1,0:T(1,128)S(1)} %bitcast.7, f32[1,512]{1,0:T(1,128)S(1)} %bitcast.10, f32[1,1024]{1,0:T(1,128)S(1)} %bitcast.8, f32[3,256]{1,0:T(4,128)S(1)} %copy-done.12, f32[3,256]{1,0:T(4,128)S(1)} %copy-done.13, ...), custom_call_target="tpu_custom_call" | custom-call | flops 8000000000 | bytes 9000000 | tf_op jit(solution)/shard_map/pallas_call | solution.py:412
  73.7 0.7 copy.24
  74.4 0.7 copy.25
  (16 shorter events, 0.0 us)
Async XLA Ops:
  1.5 1.4 %copy-start = (bf16[3,1024,256]{2,1,0:T(8,128)(2,1)S(1)}, bf16[3,1024,256]{2,1,0:T(8,128)(2,1)}, u32[]{:S(2)}) copy-start(bf16[3,1024,256]{2,1,0:T(8,128)(2,1)} %win_hbm.1) | copy-start | bytes 4718596
  2.9 1.4 %copy-start.1 = (bf16[3,1024,256]{2,1,0:T(8,128)(2,1)S(1)}, bf16[3,1024,256]{2,1,0:T(8,128)(2,1)}, u32[]{:S(2)}) copy-start(bf16[3,1024,256]{2,1,0:T(8,128)(2,1)} %whid_hbm.1) | copy-start | bytes 4718596
  4.3 1.2 %copy-start.2 = (bf16[1024,512]{1,0:T(8,128)(2,1)S(1)}, bf16[1024,512]{1,0:T(8,128)(2,1)}, u32[]{:S(2)}) copy-start(bf16[1024,512]{1,0:T(8,128)(2,1)} %feats_hbm.1) | copy-start | bytes 3145732
  5.5 1.2 %copy-start.3 = (bf16[1024,512]{1,0:T(8,128)(2,1)S(1)}, bf16[1024,512]{1,0:T(8,128)(2,1)}, u32[]{:S(2)}) copy-start(bf16[1024,512]{1,0:T(8,128)(2,1)} %wst_hbm.1) | copy-start | bytes 3145732
  6.7 1.2 %copy-start.4 = (bf16[512,1024]{1,0:T(8,128)(2,1)S(1)}, bf16[512,1024]{1,0:T(8,128)(2,1)}, u32[]{:S(2)}) copy-start(bf16[512,1024]{1,0:T(8,128)(2,1)} %wout_hbm.1) | copy-start | bytes 3145732
  8.0 1.0 %copy-start.5 = (bf16[256,1024]{1,0:T(8,128)(2,1)S(1)}, bf16[256,1024]{1,0:T(8,128)(2,1)}, u32[]{:S(2)}) copy-start(bf16[256,1024]{1,0:T(8,128)(2,1)} %mem_hbm.1) | copy-start | bytes 1572868
  9.0 1.0 %copy-start.6 = (bf16[512,512]{1,0:T(8,128)(2,1)S(1)}, bf16[512,512]{1,0:T(8,128)(2,1)}, u32[]{:S(2)}) copy-start(bf16[512,512]{1,0:T(8,128)(2,1)} %wev_hbm.1) | copy-start | bytes 1572868
  10.0 1.0 %copy-start.7 = (bf16[256,1024]{1,0:T(8,128)(2,1)S(1)}, bf16[256,1024]{1,0:T(8,128)(2,1)}, u32[]{:S(2)}) copy-start(bf16[256,1024]{1,0:T(8,128)(2,1)} %wn_hbm.1) | copy-start | bytes 1572868
  11.1 1.0 %copy-start.8 = (bf16[256,1024]{1,0:T(8,128)(2,1)S(1)}, bf16[256,1024]{1,0:T(8,128)(2,1)}, u32[]{:S(2)}) copy-start(bf16[256,1024]{1,0:T(8,128)(2,1)} %ws_hbm.1) | copy-start | bytes 1572868
  12.1 0.7 copy-start.9
  12.8 0.7 copy-start.10
  13.5 0.7 copy-start.11
  14.2 0.7 copy-start.12
  14.9 0.7 copy-start.13
  15.6 0.7 copy-start.14
  16.2 0.7 copy-start.15
  16.9 0.7 copy-start.16
  17.6 0.7 copy-start.17

commit v2 on v1

--- a/solution.py
+++ b/solution.py
@@ -11,6 +11,7 @@
 F32 = jnp.float32
 MESH = pl.DeviceIdType.MESH
 LANES = 128
+AR_CHUNKS = 4
 
 
 def iota(shape, dim):
@@ -43,12 +44,14 @@
 
 def kernel(
     n,
+    owner_hbm, slot_hbm, b_msg_hbm, b_out_hbm, b_in_hbm, b_hid_hbm,
+    sslots_hbm, neigh_hbm, query_hbm, b_emb_hbm,
+    feats_hbm, mem_hbm, wev_hbm, wst_hbm, wout_hbm, win_hbm, whid_hbm, wn_hbm, ws_hbm,
+    new_ref, emb_ref,
     owner_ref, slot_ref, b_msg_ref, b_out_ref, b_in_ref, b_hid_ref,
     sslots_ref, neigh_ref, query_ref, b_emb_ref,
-    feats_hbm, mem_hbm, wev_hbm, wst_hbm, wout_hbm, win_hbm, whid_hbm, wn_hbm, ws_hbm,
-    new_ref, emb_ref,
     feats, mem, wev, wst, wout, win, whid, wn, ws,
-    target, slotcol, send_buf, ids_send, arr, ids, proj_hi, proj_lo, gst,
+    target, slotcol, send_buf, ids_send, arr, ids, proj_ref, gst,
     acc, cnt, ar_s1, ar_r1, p_own, ar_s2, ar_r2, agg_own, agg_oth,
     smat, cmat, qmat, newm, st_send, st_recv, selfp, rs_send, rs_recv,
     load_sem, ds_sem, dr_sem, is_sem, ir_sem, xs_sem, xr_sem,
@@ -59,7 +62,7 @@
     core = m + 1 - 2 * (m % 2)
     cross = (m + 2) % 4
     far = (core + 2) % 4
-    events = owner_ref.shape[1]
+    events = owner_hbm.shape[1]
     cap = send_buf.shape[1]
     nodes = mem.shape[0]
     width = mem.shape[1]
@@ -77,11 +80,19 @@
         loads.append(c)
         return c
 
+    ld_owner = load(owner_hbm, owner_ref)
+    ld_slot = load(slot_hbm, slot_ref)
     ld_feats = load(feats_hbm.at[:, pl.ds(pl.multiple_of(m * fcols, fcols), fcols)], feats)
     ld_mem = load(mem_hbm, mem)
     ld_wst = load(wst_hbm, wst)
+    ld_b_msg = load(b_msg_hbm, b_msg_ref)
     ld_wev = load(wev_hbm, wev)
     ld_whid = load(whid_hbm, whid)
+    ld_small = [
+        load(b_hid_hbm, b_hid_ref), load(sslots_hbm, sslots_ref), load(neigh_hbm, neigh_ref),
+        load(query_hbm, query_ref), load(b_out_hbm, b_out_ref), load(b_in_hbm, b_in_ref),
+        load(b_emb_hbm, b_emb_ref),
+    ]
     ld_wout = load(wout_hbm, wout)
     ld_win = load(win_hbm, win)
     ld_ws = load(ws_hbm, ws)
@@ -97,6 +108,8 @@
     pl.semaphore_signal(barrier, inc=1, device_id=(me, core), device_id_type=MESH)
     pl.semaphore_signal(barrier, inc=1, device_id=(me, cross), device_id_type=MESH)
 
+    ld_owner.wait()
+    ld_slot.wait()
     rows = max(n, 16)
     oi = iota((rows, LANES), 0)
     tri = ones_where(iota((LANES, LANES), 0) < iota((LANES, LANES), 1)).astype(BF)
@@ -129,41 +142,6 @@
             ),
         )
 
-    def dispatch(k, c):
-        d = (me + k) % n
-        pick = ones_where(
-            target[...] == fiota((cap, events), 0) + (d * cap).astype(F32)
-        ).astype(BF)
-        out = dot(pick, jnp.concatenate([feats[...], slotcol[...]], axis=1))
-        block = out[:, :fcols].astype(BF)
-        idrow = jnp.broadcast_to(to_row(out[:, fcols:fcols + 1]), (8, cap))
-
-        @pl.when(k < n)
-        def _():
-            send_buf[d] = block
-            ids_send[d] = idrow
-            for cp in dispatch_copies(d, me):
-                cp.start()
-
-        @pl.when(k == n)
-        def _():
-            arr[m, me] = block
-            ids[me] = idrow
-
-        return c
-
-    lax.fori_loop(1, n + 1, dispatch, 0)
-
-    ld_mem.wait()
-    ld_wst.wait()
-    proj = dot(mem[...], wst[...]) + b_msg_ref[...]
-    hi = proj.astype(BF)
-    proj_hi[...] = hi
-    proj_lo[...] = (proj - hi.astype(F32)).astype(BF)
-    acc[...] = jnp.zeros_like(acc)
-    cnt[...] = jnp.zeros_like(cnt)
-    ld_wev.wait()
-
     def relay(src_col, s, to, ssem, rsem):
         return pltpu.make_async_remote_copy(
             src_ref=arr.at[src_col, s], dst_ref=arr.at[src_col, s],
@@ -171,51 +149,115 @@
             device_id=(me, to), device_id_type=MESH,
         )
 
+    mid = n // 2
+    here, place_in = me // mid, me % mid
+    there = (here + 1) % 2
+
+    def source(u):
+        far_side = u // mid
+        return ((here + far_side) % 2) * mid + (place_in - u % mid + mid) % mid
+
+    def block_for(d):
+        pick = ones_where(
+            target[...] == fiota((cap, events), 0) + (d * cap).astype(F32)
+        ).astype(BF)
+        out = dot(pick, jnp.concatenate([feats[...], slotcol[...]], axis=1))
+        idrow = jnp.broadcast_to(to_row(out[:, fcols:fcols + 1]), (8, cap))
+        return out[:, :fcols].astype(BF), idrow
+
+    def pass_on(u):
+        s = source(u)
+        relay(m, s, cross, xs_sem, xr_sem).start()
+        relay(m, s, core, c1s_sem, c1r_sem).start()
+
+    def arrive(u):
+        s = source(u)
+        for cp in dispatch_copies(s, s):
+            cp.wait_recv()
+        pass_on(u)
+
+    def forward(u):
+        s = source(u)
+        relay(cross, s, cross, xs_sem, xr_sem).wait_recv()
+        relay(cross, s, core, c2s_sem, c2r_sem).start()
+
+    def absorb(u):
+        s = source(u)
+        relay(core, s, core, c1s_sem, c1r_sem).wait_recv()
+        relay(far, s, core, c2s_sem, c2r_sem).wait_recv()
+        x = jnp.concatenate([arr[j, s] for j in range(4)], axis=1)
+        row = ids[s][0:1, :]
+        oh = ones_where(to_col(row) == fiota((cap, nodes), 1) + 1.0).astype(BF)
+        oht = ones_where(row == fiota((nodes, cap), 0) + 1.0)
+        pre = dot(x, wev[...]) + dot(oh, proj_ref[...])
+        hidden = jnp.maximum(pre, 0.0).astype(BF)
+        acc[...] += dot(oht.astype(BF), hidden)
+        cnt[...] += jnp.sum(oht, axis=1, keepdims=True)
+
+    block, idrow = block_for(me)
+    arr[m, me] = block
+    ids[me] = idrow
+    pass_on(0)
+
+    def dispatch(t, c):
+        across = t % 2
+        d = ((here + across) % 2) * mid + (place_in + t // 2) % mid
+        block, idrow = block_for(d)
+        send_buf[d] = block
+        ids_send[d] = idrow
+        for cp in dispatch_copies(d, me):
+            cp.start()
+
+        @pl.when(jnp.logical_and(t >= 4, t % 2 == 0))
+        def _():
+            arrive(t // 2 - 1)
+
+        return c
+
+    lax.fori_loop(1, n, dispatch, 0)
+
+    acc[...] = jnp.zeros_like(acc)
+    cnt[...] = jnp.zeros_like(cnt)
+    ld_mem.wait()
+    ld_wst.wait()
+    ld_b_msg.wait()
+    proj_ref[...] = (dot(mem[...], wst[...]) + b_msg_ref[...]).astype(BF)
+    ld_wev.wait()
+    ld_whid.wait()
+    for ld in ld_small:
+        ld.wait()
+
+    def each(body):
+        def run(u, c):
+            body(u)
+            return c
+
+        return run
+
+    lax.fori_loop(0, mid - 3, each(forward), 0)
+    lax.fori_loop(0, mid - 4, each(absorb), 0)
+
     def step(i, c):
         @pl.when(i < n)
         def _():
-            s = (me - i + n) % n
-
-            @pl.when(i > 0)
-            def _():
-                for cp in dispatch_copies(s, s):
-                    cp.wait_recv()
-
-            relay(m, s, cross, xs_sem, xr_sem).start()
-            relay(m, s, core, c1s_sem, c1r_sem).start()
-
-        @pl.when(jnp.logical_and(i >= 1, i <= n))
+            arrive(i)
+
+        @pl.when(i < n + 2)
         def _():
-            s = (me - i + 1 + n) % n
-            relay(cross, s, cross, xs_sem, xr_sem).wait_recv()
-            relay(cross, s, core, c2s_sem, c2r_sem).start()
-
-        @pl.when(i >= 2)
-        def _():
-            s = (me - i + 2 + n) % n
-            relay(core, s, core, c1s_sem, c1r_sem).wait_recv()
-            relay(far, s, core, c2s_sem, c2r_sem).wait_recv()
-            x = jnp.concatenate([arr[j, s] for j in range(4)], axis=1)
-            row = ids[s][0:1, :]
-            oh = ones_where(to_col(row) == fiota((cap, nodes), 1) + 1.0).astype(BF)
-            oht = ones_where(row == fiota((nodes, cap), 0) + 1.0)
-            pre = dot(x, wev[...]) + dot(oh, proj_hi[...]) + dot(oh, proj_lo[...])
-            hidden = jnp.maximum(pre, 0.0).astype(BF)
-            acc[...] += dot(oht.astype(BF), hidden)
-            cnt[...] += jnp.sum(oht, axis=1, keepdims=True)
-
-        @pl.when(i == 0)
+            forward(i - 2)
+
+        @pl.when(i == mid + 1)
         def _():
             for g in range(3):
                 gst[g] = dot(mem[...], whid[g]) + b_hid_ref[g:g + 1, :]
 
-        @pl.when(i == 1)
+        @pl.when(i == mid + 2)
         def _():
-            lane = iota((qmat.shape[0], cmat.shape[1]), 1)
-            total = jnp.zeros(cmat.shape, F32)
-            for k in range(neigh_ref.shape[1]):
-                total = total + ones_where(neigh_ref[:, k:k + 1] == lane)
-            cmat[...] = total.astype(BF)
+            place = iota((cmat.shape[1], cmat.shape[0]), 0)
+            total = jnp.zeros((cmat.shape[1], cmat.shape[0]), F32)
+            for k in range(neigh_ref.shape[0]):
+                total = total + ones_where(neigh_ref[k:k + 1, :] == place)
+            cmat[...] = total.T.astype(BF)
             qcol = to_col(query_ref[...].astype(F32))
             qmat[...] = ones_where(qcol == fiota(qmat.shape, 1)).astype(BF)
 
@@ -228,13 +270,13 @@
 
             lax.fori_loop(0, n, fill, 0)
 
-        return c
-
-    ld_whid.wait()
-    lax.fori_loop(0, n + 2, step, 0)
+        absorb(i - 3)
+        return c
+
+    lax.fori_loop(mid - 1, n + 3, step, 0)
 
     ld_wout.wait()
-    chunks = 2
+    chunks = AR_CHUNKS
     crows = nodes // chunks
     my_half = pl.ds(pl.multiple_of((m % 2) * half, half), half)
     its_half = pl.ds(pl.multiple_of((core % 2) * half, half), half)
@@ -249,11 +291,7 @@
 
     def sum_out(r, cols):
         at = pl.ds(r * crows, crows)
-        a = acc[at, :]
-        head = a.astype(BF)
-        tail = (a - head.astype(F32)).astype(BF)
-        w = wout[:, cols]
-        return dot(head, w) + dot(tail, w)
+        return dot(acc[at, :].astype(BF), wout[:, cols])
 
     stage1 = [ar_copy(0, r, ar_s1, ar_r1, core) for r in range(chunks)]
     stage2 = [ar_copy(1, r, ar_s2, ar_r2, cross) for r in range(chunks)]
@@ -332,7 +370,7 @@
 
     def embed(b):
         at = pl.ds(pl.multiple_of(b * qblock, qblock), qblock)
-        mean = (dot(cmat[at, :], st_recv[...]) / float(neigh_ref.shape[1])).astype(BF)
+        mean = (dot(cmat[at, :], st_recv[...]) / float(neigh_ref.shape[0])).astype(BF)
         return dot(mean, wn[...]) + selfp[at, :]
 
     to_core = [rs_copy(0, core), rs_copy(1, core)]
@@ -394,20 +432,24 @@
     V = pltpu.VMEM
     dma = lambda k: pltpu.SemaphoreType.DMA((k,))
     scratch = [
+        V((1, events), jnp.int32), V((1, events), jnp.int32), V((1, hid), F32),
+        V((1, width), F32), V(b_input.shape, F32), V(b_hidden.shape, F32),
+        V(state_slots.shape, jnp.int32), V(neighbours.shape[::-1], jnp.int32),
+        V((1, queries), jnp.int32), V((1, width), F32),
         V((events, fcols), BF), V(memory.shape, BF), V(w_msg_event.shape, BF),
         V(w_msg_state.shape, BF), V(w_msg_out.shape, BF), V(w_input.shape, BF),
         V(w_hidden.shape, BF), V(w_neigh.shape, BF), V(w_self.shape, BF),
         V((1, events), F32), V((events, LANES), BF), V((n, cap, fcols), BF),
         V((n, 8, cap), F32), V((4, n, cap, fcols), BF), V((n, 8, cap), F32),
-        V((nodes, hid), BF), V((nodes, hid), BF), V((3, nodes, share), F32),
+        V((nodes, hid), BF), V((3, nodes, share), F32),
         V((nodes, hid), F32), V((nodes, LANES), F32),
         V((nodes, half), BF), V((nodes, half), BF), V((nodes, half), F32),
         V((nodes, half), BF), V((nodes, half), BF), V((nodes, half), BF), V((nodes, half), BF),
         V((n * scap, nodes), BF), V((queries, n * scap), BF), V((queries, nodes), BF),
         V((nodes, share), BF), V((n * scap, share), BF), V((n * scap, share), BF),
         V((queries, width), F32), V((3, qblock, width), BF), V((3, qblock, width), BF),
-        dma(9), dma(n), dma(n), dma(n), dma(n), dma(n), dma(n),
-        dma(n), dma(n), dma(n), dma(n), dma(6), dma(6), dma(n), dma(n), dma(3), dma(3),
+        dma(19), dma(n), dma(n), dma(n), dma(n), dma(n), dma(n),
+        dma(n), dma(n), dma(n), dma(n), dma(3 * AR_CHUNKS), dma(3 * AR_CHUNKS), dma(n), dma(n), dma(3), dma(3),
     ]
     return pl.pallas_call(
         functools.partial(kernel, n),
@@ -415,16 +457,16 @@
             jax.ShapeDtypeStruct((nodes, share), BF),
             jax.ShapeDtypeStruct((qblock, width), BF),
         ),
-        in_specs=[vm] * 10 + [hbm] * 9,
+        in_specs=[hbm] * 19,
         out_specs=(vm, vm),
         scratch_shapes=scratch,
         compiler_params=pltpu.CompilerParams(
-            collective_id=0, has_side_effects=True, vmem_limit_bytes=40 * 1024 * 1024
+            collective_id=0, has_side_effects=True, vmem_limit_bytes=60 * 1024 * 1024
         ),
         cost_estimate=pl.CostEstimate(flops=8_000_000_000, bytes_accessed=9_000_000, transcendentals=0),
     )(
         event_owner.reshape(1, events), event_slot.reshape(1, events), b_msg.reshape(1, -1),
-        b_out.reshape(1, -1), b_input, b_hidden, state_slots, neighbours,
+        b_out.reshape(1, -1), b_input, b_hidden, state_slots, neighbours.T,
         query_slots.reshape(1, -1), b_embed.reshape(1, -1),
         event_feats, memory, w_msg_event, w_msg_state, w_msg_out, w_input, w_hidden,
         w_neigh, w_self,

time: 75.9 us -> 58.6 us (0.77)
  local copies, waits for them, and re-layouts: 19 us -> 3.14 us
  Pallas kernels: 55.4 us -> 54.6 us
    unnamed x39 -> x2, local copies, waits for them, and re-layouts: 19 us -> 3.14 us
    pallas_call x1, Pallas kernels: 55.4 us -> 54.6 us  [per_device(): pl.pallas_call(functools.partial(kernel, n), out_shape=(jax.ShapeDtypeStr...]
where the time goes in v2:
time: 58.6 us; the launch traced here: 58.4 us
  Pallas kernels  54.6 us (93%)
  local copies, waits for them, and re-layouts  3.14 us (5%)
  between operations  0.65 us (1%)
    pallas_call x1, Pallas kernels, per_device(): pl.pallas_call(functools.partial(kernel, n), out_shape=(jax.ShapeDtypeStr...  54.6 us
    unnamed x2, local copies, waits for them, and re-layouts  3.14 us

profile of v2, /device:TPU:0, one launch (start us, length us, event | category | flops | bytes accessed | tf_op | source)
XLA Modules:
  0.0 58.4 jit_solution(15985463604185321277)
XLA Ops:
  0.6 54.6 %shard_map.194 = (bf16[256,256]{1,0:T(8,128)(2,1)}, bf16[64,1024]{1,0:T(8,128)(2,1)}) custom-call(s32[1,1024]{1,0:T(1,128)} %bitcast.8, s32[1,1024]{1,0:T(1,128)} %bitcast.9, f32[1,512]{1,0:T(1,128)} %bitcast.12, f32[1,1024]{1,0:T(1,128)} %bitcast.10, f32[3,256]{1,0:T(4,128)} %b_in_hbm.1, f32[3,256]{1,0:T(4,128)} %b_hid_hbm.1, s32[8,32]{1,0:T(8,128)} %sslots_hbm.1, ...), custom_call_target="tpu_custom_call" | custom-call | flops 8000000000 | bytes 9000000 | tf_op jit(solution)/shard_map/pallas_call | solution.py:454
  55.3 1.6 %copy.23 = bf16[256,256]{1,0:T(8,128)(2,1)} copy(bf16[256,256]{1,0:T(8,128)(2,1)} %get-tuple-element.4) | data formatting | bytes 262144
  56.8 1.6 %copy.24 = bf16[64,1024]{1,0:T(8,128)(2,1)} copy(bf16[64,1024]{1,0:T(8,128)(2,1)} %get-tuple-element.5) | data formatting | bytes 262144

commit v3 on v2

--- a/solution.py
+++ b/solution.py
@@ -12,6 +12,7 @@
 MESH = pl.DeviceIdType.MESH
 LANES = 128
 AR_CHUNKS = 4
+VMEM_BYTES = 60 * 1024 * 1024
 
 
 def iota(shape, dim):
@@ -83,33 +84,33 @@
     ld_owner = load(owner_hbm, owner_ref)
     ld_slot = load(slot_hbm, slot_ref)
     ld_feats = load(feats_hbm.at[:, pl.ds(pl.multiple_of(m * fcols, fcols), fcols)], feats)
+
+    barrier = pltpu.get_barrier_semaphore()
+
+    def greet(k, c):
+        pl.semaphore_signal(barrier, inc=1, device_id=((me + k) % n, m), device_id_type=MESH)
+        return c
+
+    lax.fori_loop(1, n, greet, 0)
+    pl.semaphore_signal(barrier, inc=1, device_id=(me, core), device_id_type=MESH)
+    pl.semaphore_signal(barrier, inc=1, device_id=(me, cross), device_id_type=MESH)
+
+    ld_owner.wait()
+    ld_slot.wait()
     ld_mem = load(mem_hbm, mem)
     ld_wst = load(wst_hbm, wst)
     ld_b_msg = load(b_msg_hbm, b_msg_ref)
     ld_wev = load(wev_hbm, wev)
+    ld_wout = load(wout_hbm, wout)
     ld_whid = load(whid_hbm, whid)
+    ld_win = load(win_hbm, win)
     ld_small = [
         load(b_hid_hbm, b_hid_ref), load(sslots_hbm, sslots_ref), load(neigh_hbm, neigh_ref),
         load(query_hbm, query_ref), load(b_out_hbm, b_out_ref), load(b_in_hbm, b_in_ref),
         load(b_emb_hbm, b_emb_ref),
     ]
-    ld_wout = load(wout_hbm, wout)
-    ld_win = load(win_hbm, win)
     ld_ws = load(ws_hbm, ws)
     ld_wn = load(wn_hbm, wn)
-
-    barrier = pltpu.get_barrier_semaphore()
-
-    def greet(k, c):
-        pl.semaphore_signal(barrier, inc=1, device_id=((me + k) % n, m), device_id_type=MESH)
-        return c
-
-    lax.fori_loop(1, n, greet, 0)
-    pl.semaphore_signal(barrier, inc=1, device_id=(me, core), device_id_type=MESH)
-    pl.semaphore_signal(barrier, inc=1, device_id=(me, cross), device_id_type=MESH)
-
-    ld_owner.wait()
-    ld_slot.wait()
     rows = max(n, 16)
     oi = iota((rows, LANES), 0)
     tri = ones_where(iota((LANES, LANES), 0) < iota((LANES, LANES), 1)).astype(BF)
@@ -162,8 +163,7 @@
             target[...] == fiota((cap, events), 0) + (d * cap).astype(F32)
         ).astype(BF)
         out = dot(pick, jnp.concatenate([feats[...], slotcol[...]], axis=1))
-        idrow = jnp.broadcast_to(to_row(out[:, fcols:fcols + 1]), (8, cap))
-        return out[:, :fcols].astype(BF), idrow
+        return out[:, :fcols].astype(BF), to_row(out[:, fcols:fcols + 1])
 
     def pass_on(u):
         s = source(u)
@@ -186,35 +186,40 @@
         relay(core, s, core, c1s_sem, c1r_sem).wait_recv()
         relay(far, s, core, c2s_sem, c2r_sem).wait_recv()
         x = jnp.concatenate([arr[j, s] for j in range(4)], axis=1)
-        row = ids[s][0:1, :]
+        row = ids[s]
         oh = ones_where(to_col(row) == fiota((cap, nodes), 1) + 1.0).astype(BF)
         oht = ones_where(row == fiota((nodes, cap), 0) + 1.0)
         pre = dot(x, wev[...]) + dot(oh, proj_ref[...])
         hidden = jnp.maximum(pre, 0.0).astype(BF)
         acc[...] += dot(oht.astype(BF), hidden)
-        cnt[...] += jnp.sum(oht, axis=1, keepdims=True)
-
-    block, idrow = block_for(me)
-    arr[m, me] = block
-    ids[me] = idrow
-    pass_on(0)
-
-    def dispatch(t, c):
-        across = t % 2
-        d = ((here + across) % 2) * mid + (place_in + t // 2) % mid
+        for lo in range(0, cap, LANES):
+            wide = min(cap, LANES)
+            cnt[:, 0:wide] += oht[:, lo:lo + wide]
+
+    def send_block(t):
+        d = ((here + (t + 1) % 2) % 2) * mid + (place_in + t // 2) % mid
         block, idrow = block_for(d)
         send_buf[d] = block
         ids_send[d] = idrow
         for cp in dispatch_copies(d, me):
             cp.start()
 
-        @pl.when(jnp.logical_and(t >= 4, t % 2 == 0))
+    send_block(0)
+    block, idrow = block_for(me)
+    arr[m, me] = block
+    ids[me] = idrow
+    pass_on(0)
+
+    def dispatch(t, c):
+        send_block(t)
+
+        @pl.when(jnp.logical_and(t >= 5, t % 2 == 1))
         def _():
-            arrive(t // 2 - 1)
-
-        return c
-
-    lax.fori_loop(1, n, dispatch, 0)
+            arrive((t - 3) // 2)
+
+        return c
+
+    lax.fori_loop(2, n, dispatch, 0)
 
     acc[...] = jnp.zeros_like(acc)
     cnt[...] = jnp.zeros_like(cnt)
@@ -223,10 +228,6 @@
     ld_b_msg.wait()
     proj_ref[...] = (dot(mem[...], wst[...]) + b_msg_ref[...]).astype(BF)
     ld_wev.wait()
-    ld_whid.wait()
-    for ld in ld_small:
-        ld.wait()
-
     def each(body):
         def run(u, c):
             body(u)
@@ -234,46 +235,18 @@
 
         return run
 
-    lax.fori_loop(0, mid - 3, each(forward), 0)
-    lax.fori_loop(0, mid - 4, each(absorb), 0)
-
-    def step(i, c):
-        @pl.when(i < n)
-        def _():
-            arrive(i)
-
-        @pl.when(i < n + 2)
-        def _():
-            forward(i - 2)
-
-        @pl.when(i == mid + 1)
-        def _():
-            for g in range(3):
-                gst[g] = dot(mem[...], whid[g]) + b_hid_ref[g:g + 1, :]
-
-        @pl.when(i == mid + 2)
-        def _():
-            place = iota((cmat.shape[1], cmat.shape[0]), 0)
-            total = jnp.zeros((cmat.shape[1], cmat.shape[0]), F32)
-            for k in range(neigh_ref.shape[0]):
-                total = total + ones_where(neigh_ref[k:k + 1, :] == place)
-            cmat[...] = total.T.astype(BF)
-            qcol = to_col(query_ref[...].astype(F32))
-            qmat[...] = ones_where(qcol == fiota(qmat.shape, 1)).astype(BF)
-
-            def fill(d, c):
-                col = to_col(sslots_ref[pl.ds(d, 1), :].astype(F32))
-                smat[pl.ds(pl.multiple_of(d * scap, scap), scap), :] = ones_where(
-                    col == fiota((scap, nodes), 1)
-                ).astype(BF)
-                return c
-
-            lax.fori_loop(0, n, fill, 0)
-
-        absorb(i - 3)
-        return c
-
-    lax.fori_loop(mid - 1, n + 3, step, 0)
+    lax.fori_loop(0, mid - 2, each(forward), 0)
+    lax.fori_loop(0, mid - 3, each(absorb), 0)
+
+    def step(i):
+        arrive(i)
+        forward(i - 1)
+        absorb(i - 2)
+
+    lax.fori_loop(mid - 1, n, each(step), 0)
+    absorb(n - 2)
+    forward(n - 1)
+    absorb(n - 1)
 
     ld_wout.wait()
     chunks = AR_CHUNKS
@@ -308,15 +281,41 @@
         p_own[at, :] = own
         ar_s2[at, :] = own.astype(BF)
         stage2[r].start()
-    ld_win.wait()
-    for r in range(chunks):
+
+    ld_whid.wait()
+    for ld in ld_small:
+        ld.wait()
+    for g in range(3):
+        gst[g] = dot(mem[...], whid[g]) + b_hid_ref[g:g + 1, :]
+    cnt[...] = jnp.broadcast_to(jnp.sum(cnt[...], axis=1, keepdims=True), cnt.shape)
+
+    def tables():
+        place = iota((cmat.shape[1], cmat.shape[0]), 0)
+        total = jnp.zeros((cmat.shape[1], cmat.shape[0]), F32)
+        for k in range(neigh_ref.shape[0]):
+            total = total + ones_where(neigh_ref[k:k + 1, :] == place)
+        cmat[...] = total.T.astype(BF)
+        qcol = to_col(query_ref[...].astype(F32))
+        qmat[...] = ones_where(qcol == fiota(qmat.shape, 1)).astype(BF)
+
+        def fill(d, c):
+            col = to_col(sslots_ref[pl.ds(d, 1), :].astype(F32))
+            smat[pl.ds(pl.multiple_of(d * scap, scap), scap), :] = ones_where(
+                col == fiota((scap, nodes), 1)
+            ).astype(BF)
+            return c
+
+        lax.fori_loop(0, n, fill, 0)
+
+    def aggregate(r):
         at = pl.ds(r * crows, crows)
         stage2[r].wait_recv()
         total = p_own[at, :] + ar_r2[at, :].astype(F32)
         agg = total / jnp.maximum(cnt[at, :][:, 0:1], 1.0) + b_out_ref[:, my_half]
         agg_own[at, :] = agg.astype(BF)
         stage3[r].start()
-    for r in range(chunks):
+
+    def gates(r):
         at = pl.ds(r * crows, crows)
         mine = [dot(agg_own[at, :], win[g, my_half, :]) for g in range(3)]
         stage3[r].wait_recv()
@@ -333,6 +332,14 @@
         newm[at, :] = out
         new_ref[at, :] = out
 
+    aggregate(0)
+    tables()
+    ld_win.wait()
+    for r in range(1, chunks):
+        aggregate(r)
+        gates(r - 1)
+    gates(chunks - 1)
+
     def state_copy(d, s):
         return pltpu.make_async_remote_copy(
             src_ref=st_send.at[pl.ds(pl.multiple_of(d * scap, scap), scap), :],
@@ -368,26 +375,28 @@
             device_id=(me, to), device_id_type=MESH,
         )
 
-    def embed(b):
-        at = pl.ds(pl.multiple_of(b * qblock, qblock), qblock)
-        mean = (dot(cmat[at, :], st_recv[...]) / float(neigh_ref.shape[0])).astype(BF)
-        return dot(mean, wn[...]) + selfp[at, :]
+    def embed(b0, b1):
+        ats = [pl.ds(pl.multiple_of(b * qblock, qblock), qblock) for b in (b0, b1)]
+        tally = jnp.concatenate([cmat[at, :] for at in ats], axis=0)
+        mean = (dot(tally, st_recv[...]) / float(neigh_ref.shape[0])).astype(BF)
+        out = dot(mean, wn[...])
+        return out[:qblock] + selfp[ats[0], :], out[qblock:] + selfp[ats[1], :]
 
     to_core = [rs_copy(0, core), rs_copy(1, core)]
     to_cross = rs_copy(2, cross)
-    rs_send[0] = embed(far).astype(BF)
+    part0, part1 = embed(far, core)
+    rs_send[0] = part0.astype(BF)
     to_core[0].start()
-    rs_send[1] = embed(core).astype(BF)
+    rs_send[1] = part1.astype(BF)
     to_core[1].start()
-    part = embed(cross)
+    part0, part1 = embed(cross, m)
     to_core[0].wait_recv()
-    rs_send[2] = (part + rs_recv[0].astype(F32)).astype(BF)
+    rs_send[2] = (part0 + rs_recv[0].astype(F32)).astype(BF)
     to_cross.start()
-    part = embed(m)
     to_core[1].wait_recv()
-    part = part + rs_recv[1].astype(F32) + b_emb_ref[...]
+    part1 = part1 + rs_recv[1].astype(F32) + b_emb_ref[...]
     to_cross.wait_recv()
-    emb_ref[...] = jnp.maximum(part + rs_recv[2].astype(F32), 0.0).astype(BF)
+    emb_ref[...] = jnp.maximum(part1 + rs_recv[2].astype(F32), 0.0).astype(BF)
 
     def drain(s, c):
         relay(m, s, cross, xs_sem, xr_sem).wait_send()
@@ -407,6 +416,17 @@
     lax.fori_loop(1, n, drain_peers, 0)
     for cp in stage1 + stage2 + stage3 + to_core + [to_cross]:
         cp.wait_send()
+
+
+def hand_over(new_in, emb_in, new_out, emb_out, sem):
+    copies = [
+        pltpu.make_async_copy(new_in, new_out, sem.at[0]),
+        pltpu.make_async_copy(emb_in, emb_out, sem.at[1]),
+    ]
+    for c in copies:
+        c.start()
+    for c in copies:
+        c.wait()
 
 
 def per_device(
@@ -440,7 +460,7 @@
         V(w_msg_state.shape, BF), V(w_msg_out.shape, BF), V(w_input.shape, BF),
         V(w_hidden.shape, BF), V(w_neigh.shape, BF), V(w_self.shape, BF),
         V((1, events), F32), V((events, LANES), BF), V((n, cap, fcols), BF),
-        V((n, 8, cap), F32), V((4, n, cap, fcols), BF), V((n, 8, cap), F32),
+        V((n, 1, cap), F32), V((4, n, cap, fcols), BF), V((n, 1, cap), F32),
         V((nodes, hid), BF), V((3, nodes, share), F32),
         V((nodes, hid), F32), V((nodes, LANES), F32),
         V((nodes, half), BF), V((nodes, half), BF), V((nodes, half), F32),
@@ -451,7 +471,7 @@
         dma(19), dma(n), dma(n), dma(n), dma(n), dma(n), dma(n),
         dma(n), dma(n), dma(n), dma(n), dma(3 * AR_CHUNKS), dma(3 * AR_CHUNKS), dma(n), dma(n), dma(3), dma(3),
     ]
-    return pl.pallas_call(
+    results = pl.pallas_call(
         functools.partial(kernel, n),
         out_shape=(
             jax.ShapeDtypeStruct((nodes, share), BF),
@@ -461,7 +481,7 @@
         out_specs=(vm, vm),
         scratch_shapes=scratch,
         compiler_params=pltpu.CompilerParams(
-            collective_id=0, has_side_effects=True, vmem_limit_bytes=60 * 1024 * 1024
+            collective_id=0, has_side_effects=True, vmem_limit_bytes=VMEM_BYTES
         ),
         cost_estimate=pl.CostEstimate(flops=8_000_000_000, bytes_accessed=9_000_000, transcendentals=0),
     )(
@@ -471,6 +491,14 @@
         event_feats, memory, w_msg_event, w_msg_state, w_msg_out, w_input, w_hidden,
         w_neigh, w_self,
     )
+    return pl.pallas_call(
+        hand_over,
+        out_shape=[jax.ShapeDtypeStruct(r.shape, r.dtype) for r in results],
+        in_specs=[hbm, hbm],
+        out_specs=[hbm, hbm],
+        scratch_shapes=[dma(2)],
+        compiler_params=pltpu.CompilerParams(vmem_limit_bytes=VMEM_BYTES),
+    )(*results)
 
 
 def solution(mesh):

time: 58.6 us -> 65.4 us (1.12)
  Pallas kernels: 54.6 us -> 64.6 us
  local copies, waits for them, and re-layouts: 3.14 us -> 0 us
    pallas_call x0 -> x1, Pallas kernels: none -> 9.06 us  [per_device(): pl.pallas_call(hand_over, out_shape=[jax.ShapeDtypeStruct(r.shape, r.dtyp...]
    unnamed x2 -> x0, local copies, waits for them, and re-layouts: 3.14 us -> none
    pallas_call x1, Pallas kernels: 54.6 us -> 55.6 us  [per_device(): pl.pallas_call(functools.partial(kernel, n), out_shape=(jax.ShapeDtypeStr...]
where the time goes in v3:
time: 65.4 us; the launch traced here: 65.3 us
  Pallas kernels  64.6 us (99%)
    pallas_call x1, Pallas kernels, per_device(): pl.pallas_call(functools.partial(kernel, n), out_shape=(jax.ShapeDtypeStr...  55.6 us
    pallas_call x1, Pallas kernels, per_device(): pl.pallas_call(hand_over, out_shape=[jax.ShapeDtypeStruct(r.shape, r.dtyp...  9.06 us

profile of v3, /device:TPU:0, one launch (start us, length us, event | category | flops | bytes accessed | tf_op | source)
XLA Modules:
  0.0 65.3 jit_solution(2691122968781133740)
XLA Ops:
  0.6 55.6 %shard_map.194 = (bf16[256,256]{1,0:T(8,128)(2,1)}, bf16[64,1024]{1,0:T(8,128)(2,1)}) custom-call(s32[1,1024]{1,0:T(1,128)} %bitcast.8, s32[1,1024]{1,0:T(1,128)} %bitcast.9, f32[1,512]{1,0:T(1,128)} %bitcast.12, f32[1,1024]{1,0:T(1,128)} %bitcast.10, f32[3,256]{1,0:T(4,128)} %b_in_hbm.1, f32[3,256]{1,0:T(4,128)} %b_hid_hbm.1, s32[8,32]{1,0:T(8,128)} %sslots_hbm.1, ...), custom_call_target="tpu_custom_call" | custom-call | flops 8000000000 | bytes 9000000 | tf_op jit(solution)/shard_map/pallas_call | solution.py:474
  56.2 9.1 %shard_map.195 = (bf16[256,256]{1,0:T(8,128)(2,1)}, bf16[64,1024]{1,0:T(8,128)(2,1)}) custom-call(bf16[256,256]{1,0:T(8,128)(2,1)} %get-tuple-element.4.new_in, bf16[64,1024]{1,0:T(8,128)(2,1)} %get-tuple-element.5.emb_in), custom_call_target="tpu_custom_call" | custom-call | tf_op jit(solution)/shard_map/pallas_call | solution.py:494

commit v4 on v3

--- a/solution.py
+++ b/solution.py
@@ -52,7 +52,7 @@
     owner_ref, slot_ref, b_msg_ref, b_out_ref, b_in_ref, b_hid_ref,
     sslots_ref, neigh_ref, query_ref, b_emb_ref,
     feats, mem, wev, wst, wout, win, whid, wn, ws,
-    target, slotcol, send_buf, ids_send, arr, ids, proj_ref, gst,
+    target, send_buf, ids_send, arr, ids, gst,
     acc, cnt, ar_s1, ar_r1, p_own, ar_s2, ar_r2, agg_own, agg_oth,
     smat, cmat, qmat, newm, st_send, st_recv, selfp, rs_send, rs_recv,
     load_sem, ds_sem, dr_sem, is_sem, ir_sem, xs_sem, xr_sem,
@@ -64,14 +64,15 @@
     cross = (m + 2) % 4
     far = (core + 2) % 4
     events = owner_hbm.shape[1]
-    cap = send_buf.shape[1]
+    cap = ids.shape[2]
+    sc = cap // 4
     nodes = mem.shape[0]
     width = mem.shape[1]
     share = width // 4
     half = width // 2
     scap = sslots_ref.shape[1]
     qblock = emb_ref.shape[0]
-    fcols = feats.shape[1]
+    feat = feats.shape[1]
 
     loads = []
 
@@ -83,7 +84,7 @@
 
     ld_owner = load(owner_hbm, owner_ref)
     ld_slot = load(slot_hbm, slot_ref)
-    ld_feats = load(feats_hbm.at[:, pl.ds(pl.multiple_of(m * fcols, fcols), fcols)], feats)
+    ld_feats = load(feats_hbm, feats)
 
     barrier = pltpu.get_barrier_semaphore()
 
@@ -100,7 +101,7 @@
     ld_mem = load(mem_hbm, mem)
     ld_wst = load(wst_hbm, wst)
     ld_b_msg = load(b_msg_hbm, b_msg_ref)
-    ld_wev = load(wev_hbm, wev)
+    ld_wev = load(wev_hbm, wev.at[0:feat, :])
     ld_wout = load(wout_hbm, wout)
     ld_whid = load(whid_hbm, whid)
     ld_win = load(win_hbm, win)
@@ -123,24 +124,22 @@
         place = jnp.sum(match * before, axis=0, keepdims=True)
         target[:, at] = ow.astype(F32) * float(cap) + place
         running = running + jnp.sum(match, axis=1, keepdims=True)
-        col = to_col(slot_ref[:, at].astype(F32) + 1.0)
-        slotcol[at, :] = jnp.broadcast_to(col, (LANES, LANES)).astype(BF)
 
     pl.semaphore_wait(barrier, n + 1)
     ld_feats.wait()
 
-    def dispatch_copies(d, s):
-        return (
-            pltpu.make_async_remote_copy(
-                src_ref=send_buf.at[d], dst_ref=arr.at[m, s],
-                send_sem=ds_sem.at[d], recv_sem=dr_sem.at[s],
-                device_id=(d, m), device_id_type=MESH,
-            ),
-            pltpu.make_async_remote_copy(
-                src_ref=ids_send.at[d], dst_ref=ids.at[s],
-                send_sem=is_sem.at[d], recv_sem=ir_sem.at[s],
-                device_id=(d, m), device_id_type=MESH,
-            ),
+    def event_copy(d, s):
+        return pltpu.make_async_remote_copy(
+            src_ref=send_buf.at[d], dst_ref=arr.at[m, s],
+            send_sem=ds_sem.at[d], recv_sem=dr_sem.at[s],
+            device_id=(d, m), device_id_type=MESH,
+        )
+
+    def id_copy(d, s):
+        return pltpu.make_async_remote_copy(
+            src_ref=ids_send.at[d], dst_ref=ids.at[s],
+            send_sem=is_sem.at[d], recv_sem=ir_sem.at[s],
+            device_id=(d, m), device_id_type=MESH,
         )
 
     def relay(src_col, s, to, ssem, rsem):
@@ -158,12 +157,33 @@
         far_side = u // mid
         return ((here + far_side) % 2) * mid + (place_in - u % mid + mid) % mid
 
-    def block_for(d):
-        pick = ones_where(
-            target[...] == fiota((cap, events), 0) + (d * cap).astype(F32)
+    def build(half_at):
+        count = mid * sc
+        i = iota((count, 1), 0)
+        wanted = (half_at * mid + i // sc) * cap + m * sc + i % sc
+        pick = ones_where(target[...] == wanted.astype(F32)).astype(BF)
+        built = dot(pick, feats[...]).reshape(mid, sc, feat)
+        send_buf[pl.ds(half_at * mid, mid)] = built.astype(BF)
+
+    def build_ids():
+        groups = cap // 16
+        goal = target[...]
+        high = jnp.floor(goal * (1.0 / 16.0))
+        low = goal - 16.0 * high
+        slot = slot_ref[...].astype(F32) + 1.0
+        left = jnp.where(high == fiota((n * groups, events), 0), slot, 0.0).astype(BF)
+        right = ones_where(low == fiota((16, events), 0)).astype(BF)
+        digits = lax.dot_general(
+            left, right, (((1,), (1,)), ((), ())), preferred_element_type=F32
         ).astype(BF)
-        out = dot(pick, jnp.concatenate([feats[...], slotcol[...]], axis=1))
-        return out[:, :fcols].astype(BF), to_row(out[:, fcols:fcols + 1])
+        lane = iota((16, cap), 1)
+        spread = dot(digits, ones_where(lane % 16 == iota((16, cap), 0)).astype(BF))
+        wide = (n * groups, cap)
+        keep = jnp.where(iota(wide, 1) // 16 == iota(wide, 0) % groups, spread, 0.0).astype(BF)
+        tall = (rows, n * groups)
+        table = dot(ones_where(iota(tall, 1) // groups == iota(tall, 0)).astype(BF), keep)
+        for d in range(n):
+            ids_send[d] = table[d:d + 1, :]
 
     def pass_on(u):
         s = source(u)
@@ -172,8 +192,8 @@
 
     def arrive(u):
         s = source(u)
-        for cp in dispatch_copies(s, s):
-            cp.wait_recv()
+        event_copy(s, s).wait_recv()
+        id_copy(s, s).wait_recv()
         pass_on(u)
 
     def forward(u):
@@ -181,53 +201,64 @@
         relay(cross, s, cross, xs_sem, xr_sem).wait_recv()
         relay(cross, s, core, c2s_sem, c2r_sem).start()
 
-    def absorb(u):
-        s = source(u)
-        relay(core, s, core, c1s_sem, c1r_sem).wait_recv()
-        relay(far, s, core, c2s_sem, c2r_sem).wait_recv()
-        x = jnp.concatenate([arr[j, s] for j in range(4)], axis=1)
-        row = ids[s]
-        oh = ones_where(to_col(row) == fiota((cap, nodes), 1) + 1.0).astype(BF)
-        oht = ones_where(row == fiota((nodes, cap), 0) + 1.0)
-        pre = dot(x, wev[...]) + dot(oh, proj_ref[...])
-        hidden = jnp.maximum(pre, 0.0).astype(BF)
-        acc[...] += dot(oht.astype(BF), hidden)
-        for lo in range(0, cap, LANES):
-            wide = min(cap, LANES)
-            cnt[:, 0:wide] += oht[:, lo:lo + wide]
-
-    def send_block(t):
-        d = ((here + (t + 1) % 2) % 2) * mid + (place_in + t // 2) % mid
-        block, idrow = block_for(d)
-        send_buf[d] = block
-        ids_send[d] = idrow
-        for cp in dispatch_copies(d, me):
-            cp.start()
-
-    send_block(0)
-    block, idrow = block_for(me)
-    arr[m, me] = block
-    ids[me] = idrow
+    def whole(block):
+        return block if sc % 16 == 0 else block.astype(F32)
+
+    def absorb(*turns):
+        xs, ohs, ohts = [], [], []
+        for u in turns:
+            s = source(u)
+            relay(core, s, core, c1s_sem, c1r_sem).wait_recv()
+            relay(far, s, core, c2s_sem, c2r_sem).wait_recv()
+            xs += [whole(arr[j, s]) for j in range(4)]
+            row = ids[s]
+            ohs.append(ones_where(to_col(row) == fiota((cap, nodes), 1) + 1.0).astype(BF))
+            oht = ones_where(row == fiota((nodes, cap), 0) + 1.0)
+            for lo in range(0, cap, LANES):
+                wide = min(cap, LANES)
+                cnt[:, 0:wide] += oht[:, lo:lo + wide]
+            ohts.append(oht.astype(BF))
+        x = jnp.concatenate([jnp.concatenate(xs, axis=0).astype(BF), jnp.concatenate(ohs, axis=0)], axis=1)
+        hidden = jnp.maximum(dot(x, wev[...]), 0.0).astype(BF)
+        if cap % LANES == 0:
+            acc[...] += dot(jnp.concatenate(ohts, axis=1), hidden)
+        else:
+            for k, oht in enumerate(ohts):
+                acc[...] += dot(oht, hidden[k * cap:(k + 1) * cap])
+
+    build(there)
+
+    def start_there(j, c):
+        event_copy(there * mid + (place_in + j) % mid, me).start()
+        return c
+
+    lax.fori_loop(0, mid, start_there, 0)
+    build(here)
+    arr[m, me] = send_buf[me]
     pass_on(0)
 
-    def dispatch(t, c):
-        send_block(t)
-
-        @pl.when(jnp.logical_and(t >= 5, t % 2 == 1))
-        def _():
-            arrive((t - 3) // 2)
-
-        return c
-
-    lax.fori_loop(2, n, dispatch, 0)
+    def start_here(j, c):
+        event_copy(here * mid + (place_in + j) % mid, me).start()
+        return c
+
+    lax.fori_loop(1, mid, start_here, 0)
+    build_ids()
+
+    def start_ids(k, c):
+        id_copy((me + k) % n, me).start()
+        return c
+
+    lax.fori_loop(1, n, start_ids, 0)
+    ids[me] = ids_send[me]
 
     acc[...] = jnp.zeros_like(acc)
     cnt[...] = jnp.zeros_like(cnt)
     ld_mem.wait()
     ld_wst.wait()
     ld_b_msg.wait()
-    proj_ref[...] = (dot(mem[...], wst[...]) + b_msg_ref[...]).astype(BF)
+    wev[pl.ds(feat, nodes), :] = (dot(mem[...], wst[...]) + b_msg_ref[...]).astype(BF)
     ld_wev.wait()
+
     def each(body):
         def run(u, c):
             body(u)
@@ -235,16 +266,24 @@
 
         return run
 
-    lax.fori_loop(0, mid - 2, each(forward), 0)
-    lax.fori_loop(0, mid - 3, each(absorb), 0)
-
-    def step(i):
-        arrive(i)
-        forward(i - 1)
-        absorb(i - 2)
-
-    lax.fori_loop(mid - 1, n, each(step), 0)
-    absorb(n - 2)
+    lax.fori_loop(1, mid, each(arrive), 0)
+
+    def early(p):
+        forward(2 * p)
+        forward(2 * p + 1)
+        absorb(2 * p, 2 * p + 1)
+        arrive(mid + p)
+
+    def late(u):
+        forward(u - 1)
+        absorb(u - 1)
+        arrive(u)
+
+    lax.fori_loop(0, mid // 2, each(early), 0)
+    first = mid + mid // 2
+    lax.fori_loop(mid, first - 1, each(forward), 0)
+    lax.fori_loop(mid, first - 1, each(absorb), 0)
+    lax.fori_loop(first, n, each(late), 0)
     forward(n - 1)
     absorb(n - 1)
 
@@ -408,25 +447,14 @@
 
     def drain_peers(k, c):
         d = (me + k) % n
-        for cp in dispatch_copies(d, me):
-            cp.wait_send()
+        event_copy(d, me).wait_send()
+        id_copy(d, me).wait_send()
         state_copy(d, me).wait_send()
         return c
 
     lax.fori_loop(1, n, drain_peers, 0)
     for cp in stage1 + stage2 + stage3 + to_core + [to_cross]:
         cp.wait_send()
-
-
-def hand_over(new_in, emb_in, new_out, emb_out, sem):
-    copies = [
-        pltpu.make_async_copy(new_in, new_out, sem.at[0]),
-        pltpu.make_async_copy(emb_in, emb_out, sem.at[1]),
-    ]
-    for c in copies:
-        c.start()
-    for c in copies:
-        c.wait()
 
 
 def per_device(
@@ -446,7 +474,6 @@
     scap = state_slots.shape[1]
     queries = query_slots.shape[0]
     qblock = queries // shares
-    fcols = feat // shares
     vm = pl.BlockSpec(memory_space=pltpu.VMEM)
     hbm = pl.BlockSpec(memory_space=pl.ANY)
     V = pltpu.VMEM
@@ -456,12 +483,12 @@
         V((1, width), F32), V(b_input.shape, F32), V(b_hidden.shape, F32),
         V(state_slots.shape, jnp.int32), V(neighbours.shape[::-1], jnp.int32),
         V((1, queries), jnp.int32), V((1, width), F32),
-        V((events, fcols), BF), V(memory.shape, BF), V(w_msg_event.shape, BF),
+        V((events, feat), BF), V(memory.shape, BF), V((feat + nodes, hid), BF),
         V(w_msg_state.shape, BF), V(w_msg_out.shape, BF), V(w_input.shape, BF),
         V(w_hidden.shape, BF), V(w_neigh.shape, BF), V(w_self.shape, BF),
-        V((1, events), F32), V((events, LANES), BF), V((n, cap, fcols), BF),
-        V((n, 1, cap), F32), V((4, n, cap, fcols), BF), V((n, 1, cap), F32),
-        V((nodes, hid), BF), V((3, nodes, share), F32),
+        V((1, events), F32), V((n, cap // 4, feat), BF),
+        V((n, 1, cap), F32), V((4, n, cap // 4, feat), BF), V((n, 1, cap), F32),
+        V((3, nodes, share), F32),
         V((nodes, hid), F32), V((nodes, LANES), F32),
         V((nodes, half), BF), V((nodes, half), BF), V((nodes, half), F32),
         V((nodes, half), BF), V((nodes, half), BF), V((nodes, half), BF), V((nodes, half), BF),
@@ -471,7 +498,7 @@
         dma(19), dma(n), dma(n), dma(n), dma(n), dma(n), dma(n),
         dma(n), dma(n), dma(n), dma(n), dma(3 * AR_CHUNKS), dma(3 * AR_CHUNKS), dma(n), dma(n), dma(3), dma(3),
     ]
-    results = pl.pallas_call(
+    return pl.pallas_call(
         functools.partial(kernel, n),
         out_shape=(
             jax.ShapeDtypeStruct((nodes, share), BF),
@@ -491,15 +518,6 @@
         event_feats, memory, w_msg_event, w_msg_state, w_msg_out, w_input, w_hidden,
         w_neigh, w_self,
     )
-    return pl.pallas_call(
-        hand_over,
-        out_shape=[jax.ShapeDtypeStruct(r.shape, r.dtype) for r in results],
-        in_specs=[hbm, hbm],
-        out_specs=[hbm, hbm],
-        scratch_shapes=[dma(2)],
-        compiler_params=pltpu.CompilerParams(vmem_limit_bytes=VMEM_BYTES),
-    )(*results)
-
 
 def solution(mesh):
     in_specs = (

time: 65.4 us -> 64.9 us (level)
  Pallas kernels: 64.6 us -> 60.9 us
  local copies, waits for them, and re-layouts: 0 us -> 3.14 us
    pallas_call x1 -> x0, Pallas kernels: 9.06 us -> none  [per_device(): pl.pallas_call(hand_over, out_shape=[jax.ShapeDtypeStruct(r.shape, r.dtyp...]
    pallas_call x1, Pallas kernels: 55.6 us -> 60.9 us  [per_device(): pl.pallas_call(functools.partial(kernel, n), out_shape=(jax.ShapeDtypeStr...]
    unnamed x0 -> x2, local copies, waits for them, and re-layouts: none -> 3.14 us
where the time goes in v4:
time: 64.9 us; the launch traced here: 64.7 us
  Pallas kernels  60.9 us (94%)
  local copies, waits for them, and re-layouts  3.14 us (5%)
  between operations  0.65 us (1%)
    pallas_call x1, Pallas kernels, per_device(): pl.pallas_call(functools.partial(kernel, n), out_shape=(jax.ShapeDtypeStr...  60.9 us
    unnamed x2, local copies, waits for them, and re-layouts  3.14 us

profile of v4, /device:TPU:0, one launch (start us, length us, event | category | flops | bytes accessed | tf_op | source)
XLA Modules:
  0.0 64.7 jit_solution(8780380791830684094)
XLA Ops:
  0.6 60.9 %shard_map.194 = (bf16[256,256]{1,0:T(8,128)(2,1)}, bf16[64,1024]{1,0:T(8,128)(2,1)}) custom-call(s32[1,1024]{1,0:T(1,128)} %bitcast.8, s32[1,1024]{1,0:T(1,128)} %bitcast.9, f32[1,512]{1,0:T(1,128)} %bitcast.12, f32[1,1024]{1,0:T(1,128)} %bitcast.10, f32[3,256]{1,0:T(4,128)} %b_in_hbm.1, f32[3,256]{1,0:T(4,128)} %b_hid_hbm.1, s32[8,32]{1,0:T(8,128)} %sslots_hbm.1, ...), custom_call_target="tpu_custom_call" | custom-call | flops 8000000000 | bytes 9000000 | tf_op jit(solution)/shard_map/pallas_call | solution.py:501
  61.6 1.6 %copy.23 = bf16[256,256]{1,0:T(8,128)(2,1)} copy(bf16[256,256]{1,0:T(8,128)(2,1)} %get-tuple-element.4) | data formatting | bytes 262144
  63.1 1.6 %copy.24 = bf16[64,1024]{1,0:T(8,128)(2,1)} copy(bf16[64,1024]{1,0:T(8,128)(2,1)} %get-tuple-element.5) | data formatting | bytes 262144

commit v5 on v3

--- a/solution.py
+++ b/solution.py
@@ -197,14 +197,13 @@
             cnt[:, 0:wide] += oht[:, lo:lo + wide]
 
     def send_block(t):
-        d = ((here + (t + 1) % 2) % 2) * mid + (place_in + t // 2) % mid
+        d = ((here + t % 2) % 2) * mid + (place_in + t // 2) % mid
         block, idrow = block_for(d)
         send_buf[d] = block
         ids_send[d] = idrow
         for cp in dispatch_copies(d, me):
             cp.start()
 
-    send_block(0)
     block, idrow = block_for(me)
     arr[m, me] = block
     ids[me] = idrow
@@ -213,13 +212,13 @@
     def dispatch(t, c):
         send_block(t)
 
-        @pl.when(jnp.logical_and(t >= 5, t % 2 == 1))
+        @pl.when(jnp.logical_and(t >= 4, t % 2 == 0))
         def _():
-            arrive((t - 3) // 2)
-
-        return c
-
-    lax.fori_loop(2, n, dispatch, 0)
+            arrive(t // 2 - 1)
+
+        return c
+
+    lax.fori_loop(1, n, dispatch, 0)
 
     acc[...] = jnp.zeros_like(acc)
     cnt[...] = jnp.zeros_like(cnt)
@@ -235,17 +234,19 @@
 
         return run
 
-    lax.fori_loop(0, mid - 2, each(forward), 0)
-    lax.fori_loop(0, mid - 3, each(absorb), 0)
+    lax.fori_loop(0, mid - 3, each(forward), 0)
+    lax.fori_loop(0, mid - 4, each(absorb), 0)
 
     def step(i):
         arrive(i)
-        forward(i - 1)
-        absorb(i - 2)
+        forward(i - 2)
+        absorb(i - 3)
 
     lax.fori_loop(mid - 1, n, each(step), 0)
+    forward(n - 2)
+    absorb(n - 3)
+    forward(n - 1)
     absorb(n - 2)
-    forward(n - 1)
     absorb(n - 1)
 
     ld_wout.wait()
@@ -416,17 +417,6 @@
     lax.fori_loop(1, n, drain_peers, 0)
     for cp in stage1 + stage2 + stage3 + to_core + [to_cross]:
         cp.wait_send()
-
-
-def hand_over(new_in, emb_in, new_out, emb_out, sem):
-    copies = [
-        pltpu.make_async_copy(new_in, new_out, sem.at[0]),
-        pltpu.make_async_copy(emb_in, emb_out, sem.at[1]),
-    ]
-    for c in copies:
-        c.start()
-    for c in copies:
-        c.wait()
 
 
 def per_device(
@@ -471,7 +461,7 @@
         dma(19), dma(n), dma(n), dma(n), dma(n), dma(n), dma(n),
         dma(n), dma(n), dma(n), dma(n), dma(3 * AR_CHUNKS), dma(3 * AR_CHUNKS), dma(n), dma(n), dma(3), dma(3),
     ]
-    results = pl.pallas_call(
+    return pl.pallas_call(
         functools.partial(kernel, n),
         out_shape=(
             jax.ShapeDtypeStruct((nodes, share), BF),
@@ -491,15 +481,6 @@
         event_feats, memory, w_msg_event, w_msg_state, w_msg_out, w_input, w_hidden,
         w_neigh, w_self,
     )
-    return pl.pallas_call(
-        hand_over,
-        out_shape=[jax.ShapeDtypeStruct(r.shape, r.dtype) for r in results],
-        in_specs=[hbm, hbm],
-        out_specs=[hbm, hbm],
-        scratch_shapes=[dma(2)],
-        compiler_params=pltpu.CompilerParams(vmem_limit_bytes=VMEM_BYTES),
-    )(*results)
-
 
 def solution(mesh):
     in_specs = (

time: 65.4 us -> 55.8 us (0.85)
  Pallas kernels: 64.6 us -> 51.8 us
  local copies, waits for them, and re-layouts: 0 us -> 3.14 us
    pallas_call x1 -> x0, Pallas kernels: 9.06 us -> none  [per_device(): pl.pallas_call(hand_over, out_shape=[jax.ShapeDtypeStruct(r.shape, r.dtyp...]
    pallas_call x1, Pallas kernels: 55.6 us -> 51.8 us  [per_device(): pl.pallas_call(functools.partial(kernel, n), out_shape=(jax.ShapeDtypeStr...]
    unnamed x0 -> x2, local copies, waits for them, and re-layouts: none -> 3.14 us
where the time goes in v5:
time: 55.8 us; the launch traced here: 55.6 us
  Pallas kernels  51.8 us (93%)
  local copies, waits for them, and re-layouts  3.14 us (6%)
  between operations  0.65 us (1%)
    pallas_call x1, Pallas kernels, per_device(): pl.pallas_call(functools.partial(kernel, n), out_shape=(jax.ShapeDtypeStr...  51.8 us
    unnamed x2, local copies, waits for them, and re-layouts  3.14 us

profile of v5, /device:TPU:0, one launch (start us, length us, event | category | flops | bytes accessed | tf_op | source)
XLA Modules:
  0.0 55.6 jit_solution(8005151938698132480)
XLA Ops:
  0.6 51.8 %shard_map.194 = (bf16[256,256]{1,0:T(8,128)(2,1)}, bf16[64,1024]{1,0:T(8,128)(2,1)}) custom-call(s32[1,1024]{1,0:T(1,128)} %bitcast.8, s32[1,1024]{1,0:T(1,128)} %bitcast.9, f32[1,512]{1,0:T(1,128)} %bitcast.12, f32[1,1024]{1,0:T(1,128)} %bitcast.10, f32[3,256]{1,0:T(4,128)} %b_in_hbm.1, f32[3,256]{1,0:T(4,128)} %b_hid_hbm.1, s32[8,32]{1,0:T(8,128)} %sslots_hbm.1, ...), custom_call_target="tpu_custom_call" | custom-call | flops 8000000000 | bytes 9000000 | tf_op jit(solution)/shard_map/pallas_call | solution.py:464
  52.5 1.6 %copy.23 = bf16[256,256]{1,0:T(8,128)(2,1)} copy(bf16[256,256]{1,0:T(8,128)(2,1)} %get-tuple-element.4) | data formatting | bytes 262144
  54.0 1.6 %copy.24 = bf16[64,1024]{1,0:T(8,128)(2,1)} copy(bf16[64,1024]{1,0:T(8,128)(2,1)} %get-tuple-element.5) | data formatting | bytes 262144
